TPU v7x, 32 devices: a whole 2x2x4 slice. The times are simulated.
32 devices in a mesh: batch: 8 (over z, x), seq: 4 (over y, core).
Axes of the slice: x: 2, y: 2, z: 4, core: 2. Of those that a mesh axis runs over, the one named last changes fastest.
Arguments:
- tokens_in: bfloat16 [16, 2048, 768], P('batch', 'seq'), may hold values from -6 to 6
- doc_starts: int32 [16, 6], P('batch'), may hold values from 0 to 2047, as said below
- mixer_in: bfloat16 [2, 768, 1920], P(None, 'batch'), may hold values from -0.21875 to 0.21875
- mixer_out: bfloat16 [2, 768, 768], P(None, 'batch'), may hold values from -0.21875 to 0.21875
- ffn_in: bfloat16 [2, 768, 3072], P(None, 'batch'), may hold values from -0.21875 to 0.21875
- ffn_out: bfloat16 [2, 1536, 768], P(None, 'batch'), may hold values from -0.15625 to 0.15625
- gains: float32 [2, 3, 768], replicated, may hold values from 0.5 to 1.5
- gate_params: float32 [2, 2, 384], replicated, as said below
- cotangent: bfloat16 [16, 2048, 768], P('batch', 'seq'), may hold values from -6 to 6
Outputs:
- block_out: bfloat16 [16, 2048, 768], P('batch', 'seq')
- d_tokens: float32 [16, 2048, 768], P('batch', 'seq')
- d_mixer_in: float32 [2, 768, 1920], P(None, 'batch')
- d_mixer_out: float32 [2, 768, 768], P(None, 'batch')
- d_ffn_in: float32 [2, 768, 3072], P(None, 'batch')
- d_ffn_out: float32 [2, 1536, 768], P(None, 'batch')
- d_gains: float32 [2, 3, 768], replicated
- d_gate_params: float32 [2, 2, 384], replicated
Inputs may be any that keep to these rules, and one draw needn't show every extreme that they name: `doc_starts`: along each row the starts do not fall and the first is 0; equal starts mark empty documents. gate_params[l, 0] are angles, gate_params[l, 1] lower bounds of the forget gates between 0 and 1.
All inputs are finite; a program needn't handle non-finite values.
Results may differ from a plain program's by a relative error of at most 0.02.
Values may be sent and summed in bfloat16 or wider, within the bound.
A program may use at most 256 MiB of HBM per device.

v0:
```python
import functools

import jax
import jax.numpy as jnp
from jax import lax
from jax.experimental import pallas as pl
from jax.experimental.pallas import tpu as pltpu
from jax.sharding import PartitionSpec as P

EPS = 1e-06
F32 = jnp.float32
BF16 = jnp.bfloat16
LANES = 128
CHUNK = 768
MESH = pl.DeviceIdType.MESH


def sigmoid(values):
    return 1.0 / (1.0 + jnp.exp(-values))


def rms_scale(values):
    return lax.rsqrt(jnp.mean(values * values, axis=-1, keepdims=True) + EPS)


def dot(left, right):
    return jnp.dot(left, right, preferred_element_type=F32)


def dot_t(left, right):
    return lax.dot_general(left, right, (((1,), (1,)), ((), ())), preferred_element_type=F32)


def eight_sum(values):
    rows, cols = values.shape
    return jnp.sum(values.reshape(rows // 8, 8, cols), axis=0)


def wide(ref, first, last):
    return jnp.concatenate([ref[g] for g in range(first, last)], axis=-1)


def split_store(ref, first, values):
    for g in range(values.shape[1] // LANES):
        ref[first + g] = values[:, g * LANES : (g + 1) * LANES]


def lanes(values):
    return [values[:, g * LANES : (g + 1) * LANES] for g in range(values.shape[1] // LANES)]


LIMIT = 60 * 1024 * 1024


def whole(*shape):
    return pl.BlockSpec(shape, lambda *_: (0,) * len(shape), pipeline_mode=pl.Buffered(1))


def order_matrix(tokens, back):
    shape = (tokens, tokens)
    here = lax.broadcasted_iota(jnp.int32, shape, 1 if back else 0)
    there = lax.broadcasted_iota(jnp.int32, shape, 0 if back else 1)
    return jnp.where(there == (here & 7) * (tokens // 8) + (here >> 3), 1.0, 0.0).astype(BF16)


def reset_mask(rel_ref, row, first, tokens):
    here = lax.broadcasted_iota(jnp.int32, (tokens, LANES), 0)
    pos = (here & 7) * (tokens // 8) + (here >> 3) + first
    hit = pos == rel_ref[row, 0]
    for k in range(1, rel_ref.shape[1]):
        hit = hit | (pos == rel_ref[row, k])
    return hit


def retain(rel_ref, row, first, p_f, lower):
    tokens, chan = p_f.shape
    forget = sigmoid(p_f)
    lam = lower + (1.0 - lower) * forget
    keep = jnp.where(reset_mask(rel_ref, row, first, tokens), 0.0, 1.0)
    return lam * jnp.concatenate([keep] * (chan // LANES), axis=-1), forget, keep


def at_step(s):
    return pl.ds(pl.multiple_of(s * 8, 8), 8)


def enter_tile(rel_ref, row, tile, x, w_ref, gain_ref, gate_ref, proj_ref, pg_ref, normed_ref, h_ref, cum_ref,
               ends_ref, tot_ref, src, lam_ref):
    tokens, width = x.shape
    chan = width // 2
    seg = tokens // 8
    groups = chan // LANES
    normed = (x * rms_scale(x) * gain_ref[0:1, :]).astype(BF16)
    normed_ref[...] = normed
    proj = dot(normed, w_ref[...])
    proj_ref[...] = proj[:, : 3 * chan].astype(BF16)
    pg_ref[...] = proj[:, 3 * chan :].astype(BF16)
    cos, sin, lower = gate_ref[0:1, :], gate_ref[1:2, :], gate_ref[2:3, :]
    seg_cos, seg_sin = gate_ref[3:4, :], gate_ref[4:5, :]
    p_r, p_i, p_f = proj[:, :chan], proj[:, chan : 2 * chan], proj[:, 2 * chan : 3 * chan]
    lam, _, _ = retain(rel_ref, row, tile * tokens, p_f, lower)
    split_store(lam_ref, 0, lam)
    split_store(src, 0, (1.0 - lam) * (p_r * sigmoid(p_r)))
    split_store(src, groups, (1.0 - lam) * (p_i * sigmoid(p_i)))
    cos_l, sin_l = lanes(cos), lanes(sin)

    def step(s, state):
        at = at_step(s)
        after = []
        for k, (h_r, h_i, cum) in enumerate(state):
            lam_s = lam_ref[k, at, :]
            a_r, a_i = lam_s * cos_l[k], lam_s * sin_l[k]
            n_r = a_r * h_r - a_i * h_i + src[k, at, :]
            n_i = a_r * h_i + a_i * h_r + src[groups + k, at, :]
            cum = cum * lam_s
            h_ref[k, at, :] = n_r
            h_ref[groups + k, at, :] = n_i
            cum_ref[k, at, :] = cum
            after.append((n_r, n_i, cum))
        return tuple(after)

    zero = lam_ref[0, 0:8, :] * 0.0
    last = lax.fori_loop(0, seg, step, ((zero, zero, zero + 1.0),) * groups, unroll=8)
    e_r, e_i, e_c = (jnp.concatenate([v[i] for v in last], axis=-1) for i in range(3))
    ends_ref[0:8, :] = e_r
    ends_ref[8:16, :] = e_i
    ends_ref[16:24, :] = e_c

    @pl.when(tile == 0)
    def _():
        tot_ref[0:2, :] = jnp.zeros((2, chan), F32)
        tot_ref[2:3, :] = jnp.ones((1, chan), F32)

    c_r, c_i, c_l = tot_ref[0:1, :], tot_ref[1:2, :], tot_ref[2:3, :]
    for j in range(8):
        m = e_c[j : j + 1, :]
        a_r, a_i = m * seg_cos, m * seg_sin
        c_r, c_i = a_r * c_r - a_i * c_i + e_r[j : j + 1, :], a_r * c_i + a_i * c_r + e_i[j : j + 1, :]
        c_l = c_l * m
    tot_ref[0:1, :] = c_r
    tot_ref[1:2, :] = c_i
    tot_ref[2:3, :] = c_l


def leave_tile(tile, x, pg_ref, h_ref, cum_ref, ends_ref, carry_ref, wo_ref, wf_ref, wd_ref, gain_ref, gate_ref,
               starts_ref, state_ref, mixed_ref, mid_ref, normed_ref, gu_ref, hid_ref, run):
    tokens, width = x.shape
    chan = width // 2
    seg = tokens // 8
    groups = chan // LANES
    cos, sin = gate_ref[0:1, :], gate_ref[1:2, :]
    seg_cos, seg_sin = gate_ref[3:4, :], gate_ref[4:5, :]

    @pl.when(tile == 0)
    def _():
        run[0:2, :] = carry_ref[0:2, :]

    c_r, c_i = run[0:1, :], run[1:2, :]
    l_r, l_i = [], []
    for j in range(8):
        l_r.append(c_r)
        l_i.append(c_i)
        m = ends_ref[16 + j : 17 + j, :]
        a_r, a_i = m * seg_cos, m * seg_sin
        c_r, c_i = (
            a_r * c_r - a_i * c_i + ends_ref[j : j + 1, :],
            a_r * c_i + a_i * c_r + ends_ref[8 + j : 9 + j, :],
        )
    run[0:1, :] = c_r
    run[1:2, :] = c_i
    start_r, start_i = jnp.concatenate(l_r, axis=0), jnp.concatenate(l_i, axis=0)
    starts_ref[...] = jnp.concatenate([start_r, start_i], axis=-1)
    cos_l, sin_l = lanes(cos), lanes(sin)

    def step(s, state):
        at = at_step(s)
        after = []
        for k, (w_r, w_i) in enumerate(state):
            w_r, w_i = w_r * cos_l[k] - w_i * sin_l[k], w_r * sin_l[k] + w_i * cos_l[k]
            cum = cum_ref[k, at, :]
            h_ref[k, at, :] += cum * w_r
            h_ref[groups + k, at, :] += cum * w_i
            after.append((w_r, w_i))
        return tuple(after)

    lax.fori_loop(0, seg, step, tuple(zip(lanes(start_r), lanes(start_i))), unroll=8)
    state = wide(h_ref, 0, 2 * groups)
    state_ref[...] = state.astype(BF16)
    p_g = pg_ref[...].astype(F32)
    mixed = (state * rms_scale(state) * gain_ref[1:2, :] * (p_g * sigmoid(p_g))).astype(BF16)
    mixed_ref[...] = mixed
    mid = x + dot(mixed, wo_ref[...])
    mid_ref[...] = mid.astype(BF16)
    normed = (mid * rms_scale(mid) * gain_ref[2:3, :]).astype(BF16)
    normed_ref[...] = normed
    gu = dot(normed, wf_ref[...])
    gu_ref[...] = gu.astype(BF16)
    hidden = gu.shape[1] // 2
    gate = gu[:, :hidden]
    hid = (gate * sigmoid(gate) * gu[:, hidden:]).astype(BF16)
    hid_ref[...] = hid
    return mid + dot(hid, wd_ref[...])


def back_out_tile(rel_ref, row, tile, last, dx_ref, gu_ref, mid_ref, state_ref, pg_ref, pf_ref, wo_ref, wf_ref,
                  wd_ref, gain_ref, gate_ref, dz_ref, dgu_ref, dy_ref, dpg_ref, lam_ref, g_ref, cum_ref, ends_ref,
                  tot_ref, small_ref, grad):
    tokens, width = dx_ref.shape
    chan = width // 2
    seg = tokens // 8
    groups = chan // LANES
    cos, sin, lower = gate_ref[0:1, :], gate_ref[1:2, :], gate_ref[2:3, :]
    seg_cos, seg_sin = gate_ref[3:4, :], gate_ref[4:5, :]
    dx = dx_ref[...]
    dz = dx.astype(BF16)
    dz_ref[...] = dz
    d_hid = dot_t(dz, wd_ref[...])
    hidden = d_hid.shape[1]
    gate = gu_ref[:, :hidden].astype(F32)
    up = gu_ref[:, hidden:].astype(F32)
    sg = sigmoid(gate)
    silu = gate * sg
    d_gu = jnp.concatenate(
        [(d_hid * up * (sg + silu * (1.0 - sg))).astype(BF16), (d_hid * silu).astype(BF16)], axis=1
    )
    dgu_ref[...] = d_gu
    d_n = dot_t(d_gu, wf_ref[...])
    mid = mid_ref[...].astype(F32)
    scale = rms_scale(mid)
    hat = mid * scale
    d_hat = d_n * gain_ref[2:3, :]
    small_ref[16:24, :] += eight_sum(d_n * hat)
    d_mid = dx + scale * (d_hat - hat * jnp.mean(d_hat * hat, axis=-1, keepdims=True))
    dx_ref[...] = d_mid
    dy = d_mid.astype(BF16)
    dy_ref[...] = dy
    d_mixed = dot_t(dy, wo_ref[...])
    p_g = pg_ref[...].astype(F32)
    sg = sigmoid(p_g)
    silu = p_g * sg
    state = state_ref[...].astype(F32)
    scale = rms_scale(state)
    hat = state * scale
    g1 = gain_ref[1:2, :]
    dpg_ref[...] = (d_mixed * hat * g1 * (sg + silu * (1.0 - sg))).astype(BF16)
    d_n = d_mixed * silu
    small_ref[8:16, :] += eight_sum(d_n * hat)
    d_hat = d_n * g1
    split_store(grad, 0, scale * (d_hat - hat * jnp.mean(d_hat * hat, axis=-1, keepdims=True)))
    lam, _, _ = retain(rel_ref, row, tile * tokens, pf_ref[...].astype(F32), lower)
    split_store(lam_ref, 0, lam)
    cos_l, sin_l = lanes(cos), lanes(sin)

    def step(s, state):
        at = at_step(seg - 1 - s)
        after = []
        for k, (g_r, g_i, cum, lam_n) in enumerate(state):
            a_r, a_i = lam_n * cos_l[k], lam_n * sin_l[k]
            n_r = grad[k, at, :] + a_r * g_r + a_i * g_i
            n_i = grad[groups + k, at, :] + a_r * g_i - a_i * g_r
            cum = cum * lam_n
            g_ref[k, at, :] = n_r
            g_ref[groups + k, at, :] = n_i
            cum_ref[k, at, :] = cum
            after.append((n_r, n_i, cum, lam_ref[k, at, :]))
        return tuple(after)

    zero = lam_ref[0, 0:8, :] * 0.0
    final = lax.fori_loop(0, seg, step, ((zero, zero, zero + 1.0, zero + 1.0),) * groups, unroll=8)
    g_r, g_i, cum, lam_0 = (jnp.concatenate([v[i] for v in final], axis=-1) for i in range(4))
    e_r = lam_0 * (cos * g_r + sin * g_i)
    e_i = lam_0 * (cos * g_i - sin * g_r)
    e_c = lam_0 * cum
    ends_ref[0:8, :] = e_r
    ends_ref[8:16, :] = e_i
    ends_ref[16:24, :] = e_c

    @pl.when(tile == last)
    def _():
        tot_ref[0:2, :] = jnp.zeros((2, chan), F32)
        tot_ref[2:3, :] = jnp.ones((1, chan), F32)

    c_r, c_i, c_l = tot_ref[0:1, :], tot_ref[1:2, :], tot_ref[2:3, :]
    for j in reversed(range(8)):
        m = e_c[j : j + 1, :]
        a_r, a_i = m * seg_cos, m * seg_sin
        c_r, c_i = a_r * c_r + a_i * c_i + e_r[j : j + 1, :], a_r * c_i - a_i * c_r + e_i[j : j + 1, :]
        c_l = c_l * m
    tot_ref[0:1, :] = c_r
    tot_ref[1:2, :] = c_i
    tot_ref[2:3, :] = c_l


def back_in_tile(rel_ref, row, tile, last, dx_ref, x_ref, proj_ref, dpg_ref, lam_ref, starts_ref, state_ref, g_ref,
                 cum_ref, ends_ref, carry_ref, w_ref, gain_ref, gate_ref, dproj_ref, small_ref, run):
    tokens, width = dx_ref.shape
    chan = width // 2
    seg = tokens // 8
    groups = chan // LANES
    cos, sin, lower = gate_ref[0:1, :], gate_ref[1:2, :], gate_ref[2:3, :]
    seg_cos, seg_sin = gate_ref[3:4, :], gate_ref[4:5, :]

    @pl.when(tile == last)
    def _():
        run[0:2, :] = carry_ref[0:2, :]

    c_r, c_i = run[0:1, :], run[1:2, :]
    l_r, l_i = [None] * 8, [None] * 8
    for j in reversed(range(8)):
        l_r[j], l_i[j] = c_r, c_i
        m = ends_ref[16 + j : 17 + j, :]
        a_r, a_i = m * seg_cos, m * seg_sin
        c_r, c_i = (
            a_r * c_r + a_i * c_i + ends_ref[j : j + 1, :],
            a_r * c_i - a_i * c_r + ends_ref[8 + j : 9 + j, :],
        )
    run[0:1, :] = c_r
    run[1:2, :] = c_i
    cos_l, sin_l = lanes(cos), lanes(sin)

    def step(s, state):
        at = at_step(seg - 1 - s)
        after = []
        for k, (w_r, w_i) in enumerate(state):
            cum = cum_ref[k, at, :]
            g_ref[k, at, :] += cum * w_r
            g_ref[groups + k, at, :] += cum * w_i
            after.append((w_r * cos_l[k] + w_i * sin_l[k], w_i * cos_l[k] - w_r * sin_l[k]))
        return tuple(after)

    starts = (jnp.concatenate(l_r, axis=0), jnp.concatenate(l_i, axis=0))
    lax.fori_loop(0, seg, step, tuple(zip(lanes(starts[0]), lanes(starts[1]))), unroll=8)
    g_r, g_i = wide(g_ref, 0, groups), wide(g_ref, groups, 2 * groups)
    prior = jnp.concatenate([starts_ref[...], state_ref[...].astype(F32)[: tokens - 8, :]], axis=0)
    q_r, q_i = prior[:, :chan], prior[:, chan:]
    p_r = proj_ref[:, :chan].astype(F32)
    p_i = proj_ref[:, chan : 2 * chan].astype(F32)
    _, forget, keep = retain(rel_ref, row, tile * tokens, proj_ref[:, 2 * chan :].astype(F32), lower)
    lam = wide(lam_ref, 0, groups)
    d_ar = g_r * q_r + g_i * q_i
    d_ai = g_i * q_r - g_r * q_i
    s_r, s_i = sigmoid(p_r), sigmoid(p_i)
    in_r, in_i = p_r * s_r, p_i * s_i
    d_lam = d_ar * cos + d_ai * sin - (g_r * in_r + g_i * in_i)
    d_f = jnp.concatenate([keep] * groups, axis=-1) * d_lam * (1.0 - forget)
    small_ref[24:32, :] += jnp.concatenate(
        [eight_sum(lam * (d_ai * cos - d_ar * sin)), eight_sum(d_f)], axis=-1
    )
    rest = 1.0 - lam
    d_proj = jnp.concatenate(
        [
            (rest * g_r * (s_r + in_r * (1.0 - s_r))).astype(BF16),
            (rest * g_i * (s_i + in_i * (1.0 - s_i))).astype(BF16),
            (d_f * (1.0 - lower) * forget).astype(BF16),
            dpg_ref[...],
        ],
        axis=1,
    )
    dproj_ref[...] = d_proj
    d_n = dot_t(d_proj, w_ref[...])
    x = x_ref[...].astype(F32)
    scale = rms_scale(x)
    hat = x * scale
    small_ref[0:8, :] += eight_sum(d_n * hat)
    d_hat = d_n * gain_ref[0:1, :]
    dx_ref[...] = dx_ref[...] + scale * (d_hat - hat * jnp.mean(d_hat * hat, axis=-1, keepdims=True))


def combine(count, me, forward, buf, rot_ref, out_ref):
    cos, sin = rot_ref[0:1, :], rot_ref[1:2, :]
    for r in range(buf.shape[1]):
        c_r = jnp.zeros_like(cos)
        c_i = jnp.zeros_like(cos)
        for k in range(count - 1, 0, -1):
            slot = k - 1 if forward else count - k - 1
            valid = me >= k if forward else me + k < count
            e_r, e_i, m = buf[slot, r, 0:1, :], buf[slot, r, 1:2, :], buf[slot, r, 2:3, :]
            a_r = m * cos
            a_i = m * sin if forward else -m * sin
            n_r = a_r * c_r - a_i * c_i + e_r
            n_i = a_r * c_i + a_i * c_r + e_i
            keep = jnp.where(valid, 1.0, 0.0)
            c_r, c_i = n_r * keep, n_i * keep
        out_ref[r, 0:1, :] = c_r
        out_ref[r, 1:2, :] = c_i


def carry_copies(count, me, tot_ref, buf, send_sem, recv_sem):
    return [
        remote(tot_ref, buf.at[k - 1], send_sem.at[k - 1], recv_sem.at[k - 1], {"seq": lax.rem(me + k, count)})
        for k in range(1, count)
    ]


class Ring:
    def __init__(self, n):
        self.n = n
        self.batch, self.seq = lax.axis_index("batch"), lax.axis_index("seq")
        z, x = self.batch // 2, self.batch % 2
        self.pos = z + x * (n - 1 - 2 * z)
        self.core, self.y = self.seq % 2, self.seq // 2
        self.sign = 1 - 2 * self.core
        self.core_peer = self.seq + self.sign
        self.y_peer = self.seq + 2 * (1 - 2 * self.y)

    def at(self, distance):
        p = (self.pos + distance + 2 * self.n) % self.n
        h = p // (self.n // 2)
        return 2 * (p + h * (self.n - 1 - 2 * p)) + h

    def ahead(self, hops):
        return self.at(self.sign * hops)


def remote(src, dst, send, recv, device):
    return pltpu.make_async_remote_copy(
        src_ref=src, dst_ref=dst, send_sem=send, recv_sem=recv, device_id=device, device_id_type=MESH
    )


def meet(devices):
    barrier = pltpu.get_barrier_semaphore()
    for device in devices:
        pl.semaphore_signal(barrier, inc=1, device_id=device, device_id_type=MESH)
    pl.semaphore_wait(barrier, len(devices))


class Gather:
    def __init__(self, ring, jobs, sems):
        self.ring, self.jobs = ring, jobs
        (self.own_sem, self.ring_send, self.ring_recv, self.y_send, self.y_recv, self.core_send,
         self.core_recv) = sems
        n = ring.n
        self.hops = ((1, n // 2, 0), (-1, n - 1 - n // 2, n // 2))

    def rows(self, j, piece):
        src, dst, u = self.jobs[j]
        ring = self.ring
        base = ring.core * (3 * u)
        whole = piece * (6 * u)
        view = lambda first, rows: dst.at[pl.ds(pl.multiple_of(whole + base + first, 16), rows)]
        return view(ring.y * u, 2 * u), view(2 * ring.y * u, u), view(2 * (1 - ring.y) * u, u)

    def own_copy(self, j):
        src, dst, u = self.jobs[j]
        return pltpu.make_async_copy(
            src, dst.at[pl.ds(pl.multiple_of(self.ring.batch * (6 * u), 16), 6 * u)], self.own_sem.at[j]
        )

    def own(self, j):
        src, dst, u = self.jobs[j]
        ring = self.ring
        mine, _, _ = self.rows(j, ring.batch)
        piece = src.at[pl.ds(pl.multiple_of(ring.core * (3 * u) + ring.y * u, 16), 2 * u)]
        for way, hops, first in self.hops:
            remote(piece, mine, self.ring_send.at[j], self.ring_recv.at[j, first],
                   {"batch": ring.ahead(way)}).start()
        self.own_copy(j).start()

    def arrived(self, j, h):
        ring = self.ring
        for way, hops, first in self.hops:
            if h < hops:
                mine, give, _ = self.rows(j, ring.ahead(-way * (h + 1)))
                on = lambda slot: remote(mine, mine, self.ring_send.at[j], self.ring_recv.at[j, first + slot],
                                         {"batch": ring.ahead(way)})
                on(h).wait_recv()
                if h + 1 < hops:
                    on(h + 1).start()
                remote(give, give, self.y_send.at[j], self.y_recv.at[j, first + h], {"seq": ring.y_peer}).start()
                remote(mine, mine, self.core_send.at[j], self.core_recv.at[j], {"seq": ring.core_peer}).start()

    def crossed(self, j, h):
        ring = self.ring
        for way, hops, first in self.hops:
            if h < hops:
                _, _, take = self.rows(j, ring.ahead(-way * (h + 1)))
                remote(take, take, self.y_send.at[j], self.y_recv.at[j, first + h], {"seq": ring.y_peer}).wait_recv()
                remote(take, take, self.core_send.at[j], self.core_recv.at[j], {"seq": ring.core_peer}).start()

    def swapped(self, j):
        src, dst, u = self.jobs[j]
        view = dst.at[0 : (self.ring.n - 1) * 3 * u]
        remote(view, view, self.core_send.at[j], self.core_recv.at[j], {"seq": self.ring.core_peer}).wait_recv()
        self.own_copy(j).wait()

    def sent(self, j):
        src, dst, u = self.jobs[j]
        for rows, send in ((2 * u, self.ring_send), (u, self.y_send), (3 * u, self.core_send)):
            view = dst.at[0 : (self.ring.n - 1) * rows]
            remote(view, view, send.at[j], self.core_recv.at[j], {"seq": self.ring.core_peer}).wait_send()


class Agenda:
    def __init__(self):
        self.calls = {}

    def add(self, when, f, *args):
        self.calls.setdefault(when, []).append((f, args))

    def run(self, now):
        for when, calls in sorted(self.calls.items(), key=lambda item: item[0]):

            @pl.when(now == when)
            def _(calls=calls):
                for f, args in calls:
                    f(*args)


def plan_gather(agenda, net, layers, mats, count, load):
    far = net.ring.n // 2

    def hop(j, h):
        if h < far:
            net.arrived(j, h)
        if h >= 1:
            net.crossed(j, h - 1)

    def complete(j):
        net.swapped(j)
        load(j).start()

    agenda.add(0, net.own, 0)
    agenda.add(0, net.own, 1)
    for h in range(far + 1):
        agenda.add(0, hop, 0, h)
        if h == 0:
            agenda.add(0, net.own, 3)
        if h == 1:
            agenda.add(0, net.own, 2)
    agenda.add(0, complete, 0)
    for h in range(far + 1):
        for j in (1, 3, 2):
            agenda.add(min(1 + h, count), hop, j, h)
    for j in range(mats, layers * mats):
        agenda.add(max(count - 2, 0), net.own, j)
    for j in (1, 3, 2):
        agenda.add(count, complete, j)
    for k in range(1, layers):
        start = (2 * k - 1) * count
        for h in range(far + 1):
            for j in range(k * mats, k * mats + mats):
                agenda.add(start + 1 + min(h, count - 1), hop, j, h)
        agenda.add(start + count, complete, k * mats)
        for j in range(k * mats + 1, k * mats + mats):
            agenda.add(start + count + 1, complete, j)


def forward_kernel(n, n_seq, layers, rows, paired, *refs):
    rel_ref, tok_ref = refs[:2]
    mats = 4
    given, (gain_ref, gate_ref) = refs[2 : 2 + mats], refs[2 + mats : 4 + mats]
    refs = refs[4 + mats :]
    if paired:
        gathered, refs = refs[: layers * mats], refs[layers * mats :]
    (xin_ref, proj_ref, pg_ref, normed_ref, starts_ref, state_ref, mixed_ref, mid_ref, normed2_ref, gu_ref, hid_ref,
     out_ref) = refs[:12]
    (xs, hs, cum, pg, ends, tot, src, lam, run, carry, buf, *rest) = refs[12:]
    weights, (load_sem, carry_send, carry_recv), sems = rest[:mats], rest[mats : mats + 3], rest[mats + 3 :]
    layer, step = pl.program_id(0), pl.program_id(1)
    tokens = tok_ref.shape[0]
    count = xs.shape[0]
    tiles = count // rows
    now = layer * (2 * count) + step
    me = lax.axis_index("seq")
    peers = [{"seq": lax.rem(me + k, n_seq)} for k in range(1, n_seq)]
    agenda = Agenda()

    def load(j):
        source = gathered[j] if paired else given[j % mats].at[j // mats]
        return pltpu.make_async_copy(source, weights[j % mats], load_sem.at[j % mats])

    def ready(j):
        load(j).wait()

    def exchange():
        return carry_copies(n_seq, me, tot, buf.at[layer], carry_send.at[layer], carry_recv.at[layer])

    if paired:
        ring = Ring(n)
        jobs = [
            (given[m].at[k], gathered[k * mats + m], given[m].shape[1] // 6)
            for k in range(layers) for m in range(mats)
        ]
        net = Gather(ring, jobs, sems)
        agenda.add(0, meet, [{"batch": ring.ahead(1)}, {"batch": ring.ahead(-1)}] + peers)
        plan_gather(agenda, net, layers, mats, count, load)
    else:
        agenda.add(0, meet, peers)
        for k in range(layers):
            agenda.add(2 * count * k, lambda k=k: load(k * mats).start())
            for m in range(1, mats):
                agenda.add(2 * count * k + count - 1, lambda j=k * mats + m: load(j).start())
    for k in range(layers):
        agenda.add(2 * count * k, ready, k * mats)
        for m in range(1, mats):
            agenda.add(2 * count * k + count, ready, k * mats + m)
    agenda.run(now)

    tile = lax.rem(step, count)
    row, at_row = tile // tiles, lax.rem(tile, tiles)
    gains, gate = gain_ref.at[layer], gate_ref.at[layer]

    @pl.when((layer == 0) & (step < count))
    def _():
        xs[tile] = dot(order_matrix(tokens, False), tok_ref[...])

    @pl.when(step < count)
    def _():
        x = xs[tile]
        xin_ref[...] = x.astype(BF16)
        enter_tile(rel_ref, row, at_row, x, weights[0], gains, gate, proj_ref, pg.at[tile], normed_ref, hs.at[tile],
                   cum.at[tile], ends.at[tile], tot.at[row], src, lam)
        pg_ref[...] = pg[tile]

    @pl.when(step == count - 1)
    def _():
        for copy in exchange():
            copy.start()

    @pl.when(step == count)
    def _():
        for copy in exchange():
            copy.wait()
        combine(n_seq, me, True, buf.at[layer], gate.at[5:8], carry)

    @pl.when(step >= count)
    def _():
        out = leave_tile(at_row, xs[tile], pg.at[tile], hs.at[tile], cum.at[tile], ends.at[tile], carry.at[row],
                         weights[1], weights[2], weights[3], gains, gate, starts_ref, state_ref, mixed_ref, mid_ref,
                         normed2_ref, gu_ref, hid_ref, run)
        xs[tile] = out

        @pl.when(layer == layers - 1)
        def _():
            out_ref[...] = dot(order_matrix(tokens, True), out.astype(BF16)).astype(BF16)

    if paired:

        @pl.when(now == layers * 2 * count - 1)
        def _():
            for j in range(layers * mats):
                net.sent(j)


def tile_specs(tokens, layer):
    def flat(w, when, col=0):
        return pl.BlockSpec((None, tokens, w), lambda k, s: (layer(k), when(s), col))

    def few(r, w, when):
        return pl.BlockSpec((None, None, r, w), lambda k, s: (layer(k), when(s), 0, 0))

    return flat, few


def run_forward(n, n_seq, paired, rows, tokens, rel, x, sources, gain_rows, gate_rows):
    layers = sources[0].shape[0]
    total, width = x.shape
    chan = width // 2
    hidden = sources[2].shape[2] // 2
    count = total // tokens
    mats = len(sources)
    jobs = layers * mats if paired else 0
    shape = jax.ShapeDtypeStruct
    dma = pltpu.SemaphoreType.DMA
    any_ = pl.BlockSpec(memory_space=pl.ANY)

    def first(step):
        return jnp.minimum(step, count - 1)

    def second(step):
        return jnp.maximum(step - count, 0)

    flat, few = tile_specs(tokens, lambda k: k)

    def kept(w):
        return shape((layers, total, w), BF16)

    full = [((n if paired else 1) * w.shape[1], w.shape[2]) for w in sources]
    last = layers - 1
    outs = pl.pallas_call(
        functools.partial(forward_kernel, n, n_seq, layers, rows, paired),
        grid=(layers, 2 * count),
        in_specs=[
            pl.BlockSpec(memory_space=pltpu.SMEM),
            pl.BlockSpec((tokens, width), lambda k, s: (jnp.where(k == 0, first(s), count - 1), 0)),
        ]
        + [any_] * mats
        + [whole(layers, 8, width), whole(layers, 8, chan)],
        out_specs=[any_] * jobs
        + [
            flat(width, first),
            flat(3 * chan, first),
            flat(width, first),
            flat(width, first),
            few(8, width, second),
            flat(width, second),
            flat(width, second),
            flat(width, second),
            flat(width, second),
            flat(2 * hidden, second),
            flat(hidden, second),
            pl.BlockSpec((tokens, width), lambda k, s: (jnp.where(k == last, second(s), 0), 0)),
        ],
        out_shape=[shape(f, BF16) for _ in range(layers) for f in full][:jobs]
        + [
            kept(width),
            kept(3 * chan),
            kept(width),
            kept(width),
            shape((layers, count, 8, width), F32),
            kept(width),
            kept(width),
            kept(width),
            kept(width),
            kept(2 * hidden),
            kept(hidden),
            shape((total, width), BF16),
        ],
        scratch_shapes=[
            pltpu.VMEM((count, tokens, width), F32),
            pltpu.VMEM((count, width // LANES, tokens, LANES), F32),
            pltpu.VMEM((count, chan // LANES, tokens, LANES), F32),
            pltpu.VMEM((count, tokens, width), BF16),
            pltpu.VMEM((count, 24, chan), F32),
            pltpu.VMEM((rows, 8, chan), F32),
            pltpu.VMEM((width // LANES, tokens, LANES), F32),
            pltpu.VMEM((chan // LANES, tokens, LANES), F32),
            pltpu.VMEM((8, chan), F32),
            pltpu.VMEM((rows, 8, chan), F32),
            pltpu.VMEM((layers, n_seq - 1, rows, 8, chan), F32),
        ]
        + [pltpu.VMEM(f, BF16) for f in full]
        + [dma((mats,)), dma((layers, n_seq - 1)), dma((layers, n_seq - 1))]
        + [dma((s,)) if one else dma((s, n - 1)) for s in [max(jobs, 1)] for one in (1, 1, 0, 1, 0, 1, 1)],
        compiler_params=pltpu.CompilerParams(collective_id=3, has_side_effects=True, vmem_limit_bytes=LIMIT),
    )(rel, x, *sources, gain_rows, gate_rows)
    return outs[:jobs], outs[jobs:]


def backward_kernel(n_seq, layers, rows, mats, *refs):
    rel_ref, cot_ref = refs[:2]
    given, refs = refs[2 : 2 + layers * mats], refs[2 + layers * mats :]
    (gain_ref, gate_ref, gu_ref, mid_ref, state_ref, pg_ref, pf_ref, x_ref, proj_ref, starts_ref, prior_ref, dz_ref,
     dgu_ref, dy_ref, dproj_ref, dtok_ref, small_ref) = refs[:17]
    (dxs, gs, cum, lam, dpg, ends, tot, grad, run, carry, buf, *rest) = refs[17:]
    weights, (load_sem, carry_send, carry_recv) = rest[:mats], rest[mats:]
    turn, step = pl.program_id(0), pl.program_id(1)
    layer = layers - 1 - turn
    tokens = cot_ref.shape[0]
    count = dxs.shape[0]
    tiles = count // rows
    now = turn * (2 * count) + step
    me = lax.axis_index("seq")
    agenda = Agenda()

    def load(t, m):
        return pltpu.make_async_copy(given[(layers - 1 - t) * mats + m], weights[m], load_sem.at[m])

    def start(t, m):
        load(t, m).start()

    def ready(t, m):
        load(t, m).wait()

    def exchange():
        return carry_copies(n_seq, me, tot, buf.at[turn], carry_send.at[turn], carry_recv.at[turn])

    for m in (3, 2, 1):
        agenda.add(0, start, 0, m)
    agenda.add(0, meet, [{"seq": lax.rem(me + k, n_seq)} for k in range(1, n_seq)])
    for t in range(layers):
        begin = 2 * count * t
        agenda.add(begin, start, t, 0)
        for m in (3, 2, 1):
            agenda.add(begin, ready, t, m)
        agenda.add(begin + count, ready, t, 0)
        if t + 1 < layers:
            for m in (3, 2, 1):
                agenda.add(begin + count, start, t + 1, m)
    agenda.run(now)

    tile = count - 1 - lax.rem(step, count)
    row, at_row = tile // tiles, lax.rem(tile, tiles)
    gains, gate = gain_ref.at[layer], gate_ref.at[layer]

    @pl.when(step == 0)
    def _():
        small_ref[...] = jnp.zeros_like(small_ref)

    @pl.when((turn == 0) & (step < count))
    def _():
        dxs[tile] = dot(order_matrix(tokens, False), cot_ref[...])

    @pl.when(step < count)
    def _():
        back_out_tile(rel_ref, row, at_row, tiles - 1, dxs.at[tile], gu_ref, mid_ref, state_ref, pg_ref, pf_ref,
                      weights[1], weights[2], weights[3], gains, gate, dz_ref, dgu_ref, dy_ref, dpg.at[tile],
                      lam.at[tile], gs.at[tile], cum.at[tile], ends.at[tile], tot.at[row], small_ref, grad)

    @pl.when(step == count - 1)
    def _():
        for copy in exchange():
            copy.start()

    @pl.when(step == count)
    def _():
        for copy in exchange():
            copy.wait()
        combine(n_seq, me, False, buf.at[turn], gate.at[5:8], carry)

    @pl.when(step >= count)
    def _():
        back_in_tile(rel_ref, row, at_row, tiles - 1, dxs.at[tile], x_ref, proj_ref, dpg.at[tile], lam.at[tile],
                     starts_ref, prior_ref, gs.at[tile], cum.at[tile], ends.at[tile], carry.at[row], weights[0],
                     gains, gate, dproj_ref, small_ref, run)

        @pl.when(turn == layers - 1)
        def _():
            dx = dxs[tile]
            high = dx.astype(BF16)
            low = (dx - high.astype(F32)).astype(BF16)
            order = order_matrix(tokens, True)
            dtok_ref[...] = dot(order, high) + dot(order, low)


def run_backward(n_seq, rows, tokens, rel, cotangent, weights, gain_rows, gate_rows, kept):
    x, proj, p_g, starts, state, mid, gu = kept
    layers, total, width = x.shape
    chan = width // 2
    hidden = gu.shape[2] // 2
    count = total // tokens
    mats = len(weights) // layers
    shape = jax.ShapeDtypeStruct
    dma = pltpu.SemaphoreType.DMA
    any_ = pl.BlockSpec(memory_space=pl.ANY)
    last = layers - 1

    def first(step):
        return count - 1 - jnp.minimum(step, count - 1)

    def second(step):
        return count - 1 - jnp.maximum(step - count, 0)

    flat, few = tile_specs(tokens, lambda k: last - k)
    return pl.pallas_call(
        functools.partial(backward_kernel, n_seq, layers, rows, mats),
        grid=(layers, 2 * count),
        in_specs=[
            pl.BlockSpec(memory_space=pltpu.SMEM),
            pl.BlockSpec((tokens, width), lambda k, s: (jnp.where(k == 0, first(s), 0), 0)),
        ]
        + [any_] * len(weights)
        + [
            whole(layers, 8, width),
            whole(layers, 8, chan),
            flat(2 * hidden, first),
            flat(width, first),
            flat(width, first),
            flat(width, first),
            flat(chan, first, 2),
            flat(width, second),
            flat(3 * chan, second),
            few(8, width, second),
            flat(width, second),
        ],
        out_specs=[
            flat(width, first),
            flat(2 * hidden, first),
            flat(width, first),
            flat(3 * chan + width, second),
            pl.BlockSpec((tokens, width), lambda k, s: (jnp.where(k == last, second(s), count - 1), 0)),
            pl.BlockSpec((None, 32, width), lambda k, s: (last - k, 0, 0)),
        ],
        out_shape=[
            shape((layers, total, width), BF16),
            shape((layers, total, 2 * hidden), BF16),
            shape((layers, total, width), BF16),
            shape((layers, total, 3 * chan + width), BF16),
            shape((total, width), F32),
            shape((layers, 32, width), F32),
        ],
        scratch_shapes=[
            pltpu.VMEM((count, tokens, width), F32),
            pltpu.VMEM((count, width // LANES, tokens, LANES), F32),
            pltpu.VMEM((count, chan // LANES, tokens, LANES), F32),
            pltpu.VMEM((count, chan // LANES, tokens, LANES), F32),
            pltpu.VMEM((count, tokens, width), BF16),
            pltpu.VMEM((count, 24, chan), F32),
            pltpu.VMEM((rows, 8, chan), F32),
            pltpu.VMEM((width // LANES, tokens, LANES), F32),
            pltpu.VMEM((8, chan), F32),
            pltpu.VMEM((rows, 8, chan), F32),
            pltpu.VMEM((layers, n_seq - 1, rows, 8, chan), F32),
        ]
        + [pltpu.VMEM(w.shape, BF16) for w in weights[:mats]]
        + [dma((mats,)), dma((layers, n_seq - 1)), dma((layers, n_seq - 1))],
        compiler_params=pltpu.CompilerParams(collective_id=2, has_side_effects=True, vmem_limit_bytes=LIMIT),
    )(rel, cotangent, *weights, gain_rows, gate_rows, gu, mid, state, p_g, proj, x, proj, starts, state)


def add_rows(dst, dst_row, parts, rows):
    def block(i, _):
        step = pl.multiple_of(i * 16, 16)
        total = None
        for ref, first in parts:
            value = ref[pl.ds(pl.multiple_of(first + step, 16), 16), :].astype(F32)
            total = value if total is None else total + value
        dst[pl.ds(pl.multiple_of(dst_row + step, 16), 16), :] = total.astype(dst.dtype)
        return 0

    lax.fori_loop(0, rows // 16, block, 0)


def grads_kernel(n, plan, *refs):
    jobs = len(plan)
    lefts, rights, small = refs[:jobs], refs[jobs : 2 * jobs], refs[2 * jobs]
    outs_count = 1 + max(p[0] for p in plan)
    outs, small_out = refs[2 * jobs + 1 : 2 * jobs + 1 + outs_count], refs[2 * jobs + 1 + outs_count]
    rest = refs[2 * jobs + 2 + outs_count :]
    grads, core_buf, y_buf, ring_buf, fin_buf = (rest[i * jobs : (i + 1) * jobs] for i in range(5))
    (left_big, left_small, right_buf, small_buf, left_sem, right_sem, core_send, core_recv, y_send, y_recv,
     ring_send, ring_recv, end_send, end_recv, small_send, small_recv) = rest[5 * jobs :]
    ring = Ring(n)
    far, near = n // 2, n - 1 - n // 2
    core_dev, y_dev = {"seq": ring.core_peer}, {"seq": ring.y_peer}
    y, core = ring.y, ring.core
    rounds = [core_dev, y_dev]
    d = 1
    while d < n:
        rounds.append({"batch": ring.batch + d * (1 - 2 * ((ring.batch // d) % 2))})
        d *= 2
    us = [g.shape[0] // n // 6 for g in grads]
    split = [p[2] for p in plan]
    own_rows = [(2 if s else 3) * u for s, u in zip(split, us)]

    def left_copy(j):
        buf = (left_big, left_small)[j % 2]
        return pltpu.make_async_copy(lefts[j].at[plan[j][1]], buf.at[:, 0 : plan[j][3]], left_sem.at[j % 2])

    chunks = []
    for j, (_, _, _, rows, cols) in enumerate(plan):
        first = 0
        while first < cols:
            size = min(CHUNK, cols - first)
            chunks.append((j, first, size, first + size == cols))
            first += size

    def right_copy(i):
        j, first, size, _ = chunks[i]
        return pltpu.make_async_copy(
            rights[j].at[plan[j][1], :, first : first + size], right_buf.at[i % 2, :, 0:size], right_sem.at[i % 2]
        )

    left_copy(0).start()
    right_copy(0).start()
    right_copy(1).start()
    left_copy(1).start()
    meet([{"batch": ring.ahead(1)}, {"batch": ring.ahead(-1)}] + rounds)

    order = []
    for h in range(far):
        order.append((1, h, far - h))
        if h < near:
            order.append((-1, h, near - h))
    order.append((0, 0, 0))
    last = len(order)

    def rows_at(ref, first, rows):
        return ref.at[pl.ds(pl.multiple_of(first, 16), rows)]

    def core_copy(j, slot, piece):
        u = us[j]
        return remote(rows_at(grads[j], piece * (6 * u) + (1 - core) * (3 * u), 3 * u),
                      core_buf[j].at[slot], core_send.at[j], core_recv.at[j, slot], core_dev)

    def y_copy(j, slot, piece):
        u = us[j]
        src = rows_at(grads[j], piece * (6 * u) + core * (3 * u) + 2 * (1 - y) * u, u)
        return remote(src, y_buf[j].at[slot], y_send.at[j], y_recv.at[j, slot], y_dev)

    def mine(j, piece):
        u = us[j]
        return piece * (6 * u) + core * (3 * u) + (y * u if split[j] else 0)

    def ring_copy(j, slot, way, piece):
        return remote(rows_at(grads[j], mine(j, piece), own_rows[j]), ring_buf[j].at[slot], ring_send.at[j],
                      ring_recv.at[j, slot], {"batch": ring.ahead(way)})

    def small_round(r):
        return remote(small_buf.at[2 * r], small_buf.at[2 * r + 1], small_send.at[r], small_recv.at[r], rounds[r])

    small_buf[0] = small[...]
    small_round(0).start()

    def small_step(r):
        small_round(r).wait_recv()
        total = small_buf[2 * r] + small_buf[2 * r + 1]
        if r + 1 < len(rounds):
            small_buf[2 * r + 2] = total
            small_round(r + 1).start()
        else:
            small_out[...] = total

    def begin(j):
        for slot, (way, h, dist) in enumerate(order):
            core_copy(j, slot, ring.ahead(-way * dist)).start()

    def cross(j, slot):
        way, h, dist = order[slot]
        piece = ring.ahead(way * dist)
        u = us[j]
        core_copy(j, slot, piece).wait_recv()
        if not split[j]:
            return
        give = 2 * (1 - y) * u
        at = piece * (6 * u) + core * (3 * u) + give
        add_rows(grads[j], at, [(grads[j], at), (core_buf[j].at[slot], give)], u)
        y_copy(j, slot, piece).start()

    def hop(j, slot):
        way, h, dist = order[slot]
        piece = ring.ahead(way * dist)
        u = us[j]
        if split[j]:
            y_copy(j, slot, piece).wait_recv()
        if way == 0:
            prior = [i for i, o in enumerate(order) if o[2] == 1]
        elif h:
            prior = [i for i, o in enumerate(order) if o[0] == way and o[1] == h - 1]
        else:
            prior = []
        for i in prior:
            ring_copy(j, i, order[i][0], piece).wait_recv()
        at = mine(j, piece)
        base = [(grads[j], at), (core_buf[j].at[slot], y * u if split[j] else 0)]
        base += [(ring_buf[j].at[i], 0) for i in prior]
        if split[j]:
            for by, more in ((y * u, [(y_buf[j].at[slot], 0)]), ((1 - y) * u, [])):
                add_rows(grads[j], at + by, [(r, f + by) for r, f in base] + more, u)
        else:
            add_rows(grads[j], at, base, 3 * u)
        if way:
            ring_copy(j, slot, way, piece).start()

    def fin_copy(j):
        return remote(rows_at(grads[j], mine(j, ring.batch), own_rows[j]), fin_buf[j], end_send.at[j, 0],
                      end_recv.at[j, 0], y_dev)

    def half_copy(j):
        half = outs[plan[j][0]].at[plan[j][1], pl.ds(pl.multiple_of(core * (3 * us[j]), 16), 3 * us[j])]
        return remote(half, half, end_send.at[j, 1], end_recv.at[j, 1], core_dev)

    def finish(j):
        u = us[j]
        fin_copy(j).wait_recv()
        out = outs[plan[j][0]].at[plan[j][1]]
        at, to = mine(j, ring.batch), core * (3 * u)
        if split[j]:
            add_rows(out, to + 2 * y * u, [(grads[j], at + y * u)], u)
            add_rows(out, to + 2 * (1 - y) * u, [(fin_buf[j], (1 - y) * u)], u)
            add_rows(out, to + u, [(grads[j], at + (1 - y) * u), (fin_buf[j], y * u)], u)
        else:
            add_rows(out, to, [(grads[j], at), (fin_buf[j], 0)], 3 * u)
        half_copy(j).start()

    steps = far + 4

    def advance(j, t):
        now = [i for i, o in enumerate(order) if o[0] and o[1] == t]
        before = [i for i, o in enumerate(order) if o[0] and o[1] == t - 1]
        for slot in before:
            hop(j, slot)
        for slot in now:
            cross(j, slot)
        if t == far - 1:
            cross(j, last - 1)
        if t == far + 1:
            hop(j, last - 1)
            fin_copy(j).start()
        if t == far + 2:
            finish(j)
        if t == far + 3:
            half_copy(j).wait_recv()

    stage = {}

    def advance_all(turn):
        for j in list(stage):
            if j % 2 == turn:
                advance(j, stage[j])
                stage[j] += 1
                if stage[j] == steps:
                    del stage[j]

    small_at = 0
    for i, (j, first, size, done) in enumerate(chunks):
        if first == 0:
            left_copy(j).wait()
        right_copy(i).wait()
        left = (left_big, left_small)[j % 2]

        def multiply(b, _, i=i, j=j, first=first, size=size, left=left):
            at = pl.multiple_of(b * 256, 256)
            part = lax.dot_general(
                left[:, pl.ds(at, 256)], right_buf[i % 2, :, 0:size], (((0,), (0,)), ((), ())),
                preferred_element_type=F32,
            )
            grads[j][pl.ds(at, 256), first : first + size] = part.astype(BF16)
            return 0

        lax.fori_loop(0, plan[j][3] // 256, multiply, 0)
        if i + 2 < len(chunks):
            right_copy(i + 2).start()
        if done and j + 2 < jobs:
            left_copy(j + 2).start()
        advance_all(i % 2)
        if done:
            begin(j)
            stage[j] = 0
        if small_at < len(rounds):
            small_step(small_at)
            small_at += 1
    i = 0
    while stage:
        advance_all(i % 2)
        i += 1
    while small_at < len(rounds):
        small_step(small_at)
        small_at += 1
    for j in range(jobs):
        u = us[j]
        fin_copy(j).wait_send()
        half_copy(j).wait_send()
        remote(core_buf[j], core_buf[j], core_send.at[j], core_recv.at[j, 0], core_dev).wait_send()
        if split[j]:
            remote(y_buf[j], y_buf[j], y_send.at[j], y_recv.at[j, 0], y_dev).wait_send()
        remote(ring_buf[j], ring_buf[j], ring_send.at[j], ring_recv.at[j, 0], core_dev).wait_send()
    for r in range(len(rounds)):
        small_round(r).wait_send()


def grads_and_scatter(n, plan, lefts, rights, small):
    jobs = len(plan)
    plan = [p + (a.shape[2], b.shape[2]) for p, a, b in zip(plan, lefts, rights)]
    tokens = lefts[0].shape[1]
    layers = 1 + max(p[1] for p in plan)
    dma = pltpu.SemaphoreType.DMA
    rounds = 2 + (n - 1).bit_length()
    sizes = [(p[3] // n // 6, p[4], p[2]) for p in plan]
    outs = {p[0]: jax.ShapeDtypeStruct((layers, p[3] // n, p[4]), BF16) for p in plan}
    vm = pl.BlockSpec(memory_space=pltpu.VMEM)
    any_ = pl.BlockSpec(memory_space=pl.ANY)

    def bufs(f):
        return [pltpu.VMEM(f(u, w, s), BF16) for u, w, s in sizes]

    return pl.pallas_call(
        functools.partial(grads_kernel, n, plan),
        out_shape=[outs[m] for m in sorted(outs)] + [jax.ShapeDtypeStruct(small.shape, F32)],
        in_specs=[any_] * (2 * jobs) + [vm],
        out_specs=[vm] * (len(outs) + 1),
        scratch_shapes=bufs(lambda u, w, s: (6 * u * n, w))
        + bufs(lambda u, w, s: (n, 3 * u, w))
        + bufs(lambda u, w, s: (n if s else 1, u, w))
        + bufs(lambda u, w, s: (n - 1, 2 * u if s else 3 * u, w))
        + bufs(lambda u, w, s: (2 * u if s else 3 * u, w))
        + [
            pltpu.VMEM((tokens, max(p[3] for p in plan[0::2])), BF16),
            pltpu.VMEM((tokens, max(p[3] for p in plan[1::2])), BF16),
            pltpu.VMEM((2, tokens, CHUNK), BF16),
            pltpu.VMEM((2 * rounds,) + small.shape, F32),
            dma((2,)), dma((2,)), dma((jobs,)), dma((jobs, n)), dma((jobs,)), dma((jobs, n)), dma((jobs,)),
            dma((jobs, n)), dma((jobs, 2)), dma((jobs, 2)), dma((rounds,)), dma((rounds,)),
        ],
        compiler_params=pltpu.CompilerParams(
            collective_id=4, has_side_effects=True, vmem_limit_bytes=63 * 1024 * 1024
        ),
    )(*lefts, *rights, small)


def contract_rows(left, right):
    return lax.dot_general(
        left, right, (((0,), (0,)), ((), ())), preferred_element_type=F32
    ).astype(BF16)


def shards(
    tokens_in, doc_starts, mixer_in, mixer_out, ffn_in, ffn_out, gains, gate_params, cotangent
):
    rows, length, width = tokens_in.shape
    layers = gains.shape[0]
    chan = width // 2
    total = rows * length
    tokens = min(length, 256)
    seg = tokens // 8
    n, n_seq = lax.axis_size("batch"), lax.axis_size("seq")
    sources = (mixer_in, mixer_out, ffn_in, ffn_out)
    paired = n_seq == 4 and n % 4 == 0 and all(w.shape[1] % 96 == 0 for w in sources)
    rel = doc_starts - lax.axis_index("seq") * length
    gain_rows = jnp.pad(gains, ((0, 0), (0, 5), (0, 0)))
    theta, lower = gate_params[:, 0], gate_params[:, 1]
    turns = jnp.stack([theta, theta * seg, theta * length], axis=1)
    cos, sin = jnp.cos(turns), jnp.sin(turns)
    gate_rows = jnp.stack(
        [cos[:, 0], sin[:, 0], lower, cos[:, 1], sin[:, 1], cos[:, 2], sin[:, 2], lower], axis=1
    )
    x = tokens_in.reshape(total, width)
    if paired:
        weights, kept = run_forward(n, n_seq, True, rows, tokens, rel, x, sources, gain_rows, gate_rows)
    else:
        stacked = [lax.all_gather(w, "batch", axis=1, tiled=True) for w in sources]
        weights = [w[k] for k in range(layers) for w in stacked]
        _, kept = run_forward(n, n_seq, False, rows, tokens, rel, x, stacked, gain_rows, gate_rows)
    x_in, proj, p_g, normed, starts, state, mixed, mid, normed2, gu, hid, block_out = kept
    dz, d_gu, dy, d_proj, d_tokens, small = run_backward(
        n_seq, rows, tokens, rel, cotangent.reshape(total, width), weights, gain_rows, gate_rows,
        (x_in, proj, p_g, starts, state, mid, gu),
    )
    small = jnp.sum(small.reshape(layers, 4, 8, width), axis=2).reshape(layers * 4, width)
    pairs = ((normed, d_proj), (mixed, dy), (normed2, d_gu), (hid, dz))
    if paired:
        plan = []
        for k in reversed(range(layers)):
            plan += [(m, k, m != 0) for m in ((1, 2, 3, 0) if k == layers - 1 else (3, 2, 0, 1))]
        *outs, totals = grads_and_scatter(
            n, plan, [pairs[m][0] for m, _, _ in plan], [pairs[m][1] for m, _, _ in plan], small
        )
    else:
        outs = []
        for left, right in pairs:
            whole_grads = jnp.stack([contract_rows(left[k], right[k]) for k in range(layers)])
            part = lax.psum_scatter(whole_grads, "batch", scatter_dimension=1, tiled=True)
            outs.append(lax.psum(part, "seq"))
        totals = lax.psum(small, ("batch", "seq"))
    totals = totals.reshape(layers, 4, width)
    return (
        block_out.reshape(rows, length, width),
        d_tokens.reshape(rows, length, width),
        *[o.astype(F32) for o in outs],
        totals[:, :3],
        totals[:, 3].reshape(layers, 2, chan),
    )


def solution(mesh):
    tok = P("batch", "seq", None)
    mat = P(None, "batch", None)
    return jax.shard_map(
        shards,
        mesh=mesh,
        in_specs=(tok, P("batch", None), mat, mat, mat, mat, P(), P(), tok),
        out_specs=(tok, tok, mat, mat, mat, mat, P(), P()),
        check_vma=False,
    )
```

profile of v0, /device:TPU:0, one launch (start us, length us, event | category | flops | bytes accessed | tf_op | source)
XLA Modules:
  0.0 348.7 jit_solution(563463529087758261)
XLA Ops:
  0.6 1.2 broadcast_subtract_fusion.refs_0_
  1.9 0.8 fusion.4
  2.7 0.7 copy.17
  3.4 0.6 pad.4.refs_6_.refs_10_
  4.0 0.1 fusion
  4.2 0.7 stack.9.refs_7_.refs_11_
  4.8 144.1 %shard_map.152 = (bf16[768,1920]{1,0:T(8,128)(2,1)}, bf16[768,768]{1,0:T(8,128)(2,1)}, bf16[768,3072]{1,0:T(8,128)(2,1)}, bf16[1536,768]{1,0:T(8,128)(2,1)}, bf1...) custom-call(s32[2,6]{1,0:T(2,128)} %broadcast_subtract_fusion.refs_0, ...), custom_call_target="tpu_custom_call" | custom-call | tf_op jit(solution)/shard_map/pallas_call | solution.py:681
  148.9 69.9 %shard_map.153 = (bf16[2,1024,768]{2,1,0:T(8,128)(2,1)}, bf16[2,1024,3072]{2,1,0:T(8,128)(2,1)}, bf16[2,1024,768]{2,1,0:T(8,128)(2,1)}, bf16[2,1024,1920]{2,1,0:...) custom-call(s32[2,6]{1,0:T(2,128)} %broadcast_subtract_fusion.refs_0_, bf16[1024,768]{1,0:T(8,128)(2,1)} %bitcast.10, ...), custom_call_target="tpu_custom_call" | custom-call | tf_op jit(solution)/shard_map/pallas_call | solution.py:846
  218.8 1.0 bitcast_reduce_fusion
  219.8 0.6 reshape.42.refs_16_
  220.5 116.0 %shard_map.154 = (bf16[2,96,1920]{2,1,0:T(8,128)(2,1)}, bf16[2,96,768]{2,1,0:T(8,128)(2,1)}, bf16[2,96,3072]{2,1,0:T(8,128)(2,1)}, bf16[2,192,768]{2,1,0:T(8,128)(2,1)}, f32[8,768]{1,0:T(8,128)}) custom-call(bf16[2,1024,768]{2,1,0:T(8,128)(2,1)} %get-tuple-element.56.refs_0_.refs_7_, bf16[2,1024,768]{2,1,0:T(8,128)(2,1)} %get-tuple-element.57.refs_1_.refs_5_, ...), custom_call_target="tpu_custom_call" | custom-call | tf_op jit(solution)/shard_map/pallas_call | solution.py:1158
  336.5 0.0 copy-start.3
  336.5 0.0 copy-start.2
  336.5 0.9 reshape.43
  337.4 0.6 reshape_squeeze.3
  338.1 0.6 copy.19
  338.7 1.8 convert_element_type.15
  340.5 2.3 convert_element_type.14
  342.8 0.0 copy-done.3
  342.8 1.1 convert_element_type.17
  343.9 1.7 convert_element_type.16
  345.6 1.1 copy.22
  346.7 0.3 copy-done
  347.0 1.7 copy.23
  (6 shorter events, 0.1 us)
Async XLA Ops:
  336.5 6.3 %copy-start.3 = (bf16[2,192,768]{2,1,0:T(8,128)(2,1)S(1)}, bf16[2,192,768]{2,1,0:T(8,128)(2,1)}, u32[]{:S(2)}) copy-start(bf16[2,192,768]{2,1,0:T(8,128)(2,1)} %get-tuple-element.68) | copy-start | bytes 1769476
  336.5 7.4 %copy-start.2 = (bf16[2,96,3072]{2,1,0:T(8,128)(2,1)S(1)}, bf16[2,96,3072]{2,1,0:T(8,128)(2,1)}, u32[]{:S(2)}) copy-start(bf16[2,96,3072]{2,1,0:T(8,128)(2,1)} %get-tuple-element.67) | copy-start | bytes 3538948
  342.8 2.8 copy-start.1
  343.9 3.1 copy-start
where the time goes:
time: 349 us
  Pallas kernels  330 us (95%)
  other arithmetic  10 us (3%)
  local copies, waits for them, and re-layouts  7.93 us (2%)
    pallas_call x1, Pallas kernels, run_forward(): pl.pallas_call(functools.partial(forward_kernel, n, n_seq, layers, rows,...  144 us
    pallas_call x1, Pallas kernels, grads_and_scatter(): pl.pallas_call(functools.partial(grads_kernel, n, plan), out_shape=[outs[...  116 us
    pallas_call x1, Pallas kernels, run_backward(): pl.pallas_call(functools.partial(backward_kernel, n_seq, layers, rows, ma...  69.9 us

commit v1 on v0

--- a/solution.py
+++ b/solution.py
@@ -78,6 +78,15 @@
     lam = lower + (1.0 - lower) * forget
     keep = jnp.where(reset_mask(rel_ref, row, first, tokens), 0.0, 1.0)
     return lam * jnp.concatenate([keep] * (chan // LANES), axis=-1), forget, keep
+
+
+def pieces(total):
+    size = 512 if total % 512 == 0 else total
+    return [slice(first, first + size) for first in range(0, total, size)]
+
+
+def moved(part, by):
+    return slice(part.start + by, part.stop + by)
 
 
 def at_step(s):
@@ -92,14 +101,16 @@
     groups = chan // LANES
     normed = (x * rms_scale(x) * gain_ref[0:1, :]).astype(BF16)
     normed_ref[...] = normed
-    proj = dot(normed, w_ref[...])
-    proj_ref[...] = proj[:, : 3 * chan].astype(BF16)
-    pg_ref[...] = proj[:, 3 * chan :].astype(BF16)
+    p_f = dot(normed, w_ref[:, 2 * chan : 3 * chan])
+    p_c = dot(normed, w_ref[:, : 2 * chan])
+    proj_ref[:, 2 * chan :] = p_f.astype(BF16)
     cos, sin, lower = gate_ref[0:1, :], gate_ref[1:2, :], gate_ref[2:3, :]
     seg_cos, seg_sin = gate_ref[3:4, :], gate_ref[4:5, :]
-    p_r, p_i, p_f = proj[:, :chan], proj[:, chan : 2 * chan], proj[:, 2 * chan : 3 * chan]
     lam, _, _ = retain(rel_ref, row, tile * tokens, p_f, lower)
     split_store(lam_ref, 0, lam)
+    pg_ref[...] = dot(normed, w_ref[:, 3 * chan :]).astype(BF16)
+    proj_ref[:, : 2 * chan] = p_c.astype(BF16)
+    p_r, p_i = p_c[:, :chan], p_c[:, chan:]
     split_store(src, 0, (1.0 - lam) * (p_r * sigmoid(p_r)))
     split_store(src, groups, (1.0 - lam) * (p_i * sigmoid(p_i)))
     cos_l, sin_l = lanes(cos), lanes(sin)
@@ -193,13 +204,21 @@
     mid_ref[...] = mid.astype(BF16)
     normed = (mid * rms_scale(mid) * gain_ref[2:3, :]).astype(BF16)
     normed_ref[...] = normed
-    gu = dot(normed, wf_ref[...])
-    gu_ref[...] = gu.astype(BF16)
-    hidden = gu.shape[1] // 2
-    gate = gu[:, :hidden]
-    hid = (gate * sigmoid(gate) * gu[:, hidden:]).astype(BF16)
-    hid_ref[...] = hid
-    return mid + dot(hid, wd_ref[...])
+    hidden = wd_ref.shape[0]
+    parts = pieces(hidden)
+
+    def gate_up(part):
+        return dot(normed, wf_ref[:, part]), dot(normed, wf_ref[:, moved(part, hidden)])
+
+    after = gate_up(parts[0])
+    for i, part in enumerate(parts):
+        gate, up = after
+        if i + 1 < len(parts):
+            after = gate_up(parts[i + 1])
+        gu_ref[:, part] = gate.astype(BF16)
+        gu_ref[:, moved(part, hidden)] = up.astype(BF16)
+        hid_ref[:, part] = (gate * sigmoid(gate) * up).astype(BF16)
+    return mid + dot(hid_ref[...], wd_ref[...])
 
 
 def back_out_tile(rel_ref, row, tile, last, dx_ref, gu_ref, mid_ref, state_ref, pg_ref, pf_ref, wo_ref, wf_ref,
@@ -214,17 +233,20 @@
     dx = dx_ref[...]
     dz = dx.astype(BF16)
     dz_ref[...] = dz
-    d_hid = dot_t(dz, wd_ref[...])
-    hidden = d_hid.shape[1]
-    gate = gu_ref[:, :hidden].astype(F32)
-    up = gu_ref[:, hidden:].astype(F32)
-    sg = sigmoid(gate)
-    silu = gate * sg
-    d_gu = jnp.concatenate(
-        [(d_hid * up * (sg + silu * (1.0 - sg))).astype(BF16), (d_hid * silu).astype(BF16)], axis=1
-    )
-    dgu_ref[...] = d_gu
-    d_n = dot_t(d_gu, wf_ref[...])
+    hidden = wd_ref.shape[0]
+    parts = pieces(hidden)
+    d_next = dot_t(dz, wd_ref[parts[0], :])
+    for i, part in enumerate(parts):
+        d_hid = d_next
+        if i + 1 < len(parts):
+            d_next = dot_t(dz, wd_ref[parts[i + 1], :])
+        gate = gu_ref[:, part].astype(F32)
+        up = gu_ref[:, moved(part, hidden)].astype(F32)
+        sg = sigmoid(gate)
+        silu = gate * sg
+        dgu_ref[:, part] = (d_hid * up * (sg + silu * (1.0 - sg))).astype(BF16)
+        dgu_ref[:, moved(part, hidden)] = (d_hid * silu).astype(BF16)
+    d_n = dot_t(dgu_ref[...], wf_ref[...])
     mid = mid_ref[...].astype(F32)
     scale = rms_scale(mid)
     hat = mid * scale
@@ -330,6 +352,7 @@
 
     starts = (jnp.concatenate(l_r, axis=0), jnp.concatenate(l_i, axis=0))
     lax.fori_loop(0, seg, step, tuple(zip(lanes(starts[0]), lanes(starts[1]))), unroll=8)
+    d_n = dot_t(dpg_ref[...], w_ref[:, 3 * chan :])
     g_r, g_i = wide(g_ref, 0, groups), wide(g_ref, groups, 2 * groups)
     prior = jnp.concatenate([starts_ref[...], state_ref[...].astype(F32)[: tokens - 8, :]], axis=0)
     q_r, q_i = prior[:, :chan], prior[:, chan:]
@@ -352,12 +375,12 @@
             (rest * g_r * (s_r + in_r * (1.0 - s_r))).astype(BF16),
             (rest * g_i * (s_i + in_i * (1.0 - s_i))).astype(BF16),
             (d_f * (1.0 - lower) * forget).astype(BF16),
-            dpg_ref[...],
         ],
         axis=1,
     )
-    dproj_ref[...] = d_proj
-    d_n = dot_t(d_proj, w_ref[...])
+    dproj_ref[:, : 3 * chan] = d_proj
+    dproj_ref[:, 3 * chan :] = dpg_ref[...]
+    d_n = d_n + dot_t(d_proj, w_ref[:, : 3 * chan])
     x = x_ref[...].astype(F32)
     scale = rms_scale(x)
     hat = x * scale
@@ -507,43 +530,58 @@
                     f(*args)
 
 
+OPENING = (((0, 0, 0), (0, 0, 1), (0, 0, 3), (0, 0, 2), (1, 0, 0), (1, 0, 1), (1, 0, 3), (1, 0, 2), (2, 0, 0), (2, 0, 1),
+            (2, 0, 3), (2, 0, 2), (3, 0, 0), (3, 0, 1), (3, 0, 3), (4, 0, 0), (3, 0, 2), (0, 1, 0), (0, 1, 1), (0, 1, 3),
+            (5, 0, 0)),)
+FIRST = OPENING + (
+    ((4, 0, 1), (4, 0, 3), (0, 1, 2)),
+    ((4, 0, 2), (1, 1, 0)),
+    ((5, 0, 1), (5, 0, 3), (1, 1, 1), (1, 1, 3)),
+    ((5, 0, 2), (1, 1, 2)),
+)
+SECOND = (
+    ((2, 1, 0), (2, 1, 1), (2, 1, 3)),
+    ((2, 1, 2), (3, 1, 0)),
+    ((3, 1, 1), (3, 1, 3), (4, 1, 0)),
+)
+LATER = (
+    ((5, 0, 0), (3, 0, 2)),
+    ((4, 0, 1), (4, 0, 3), (0, 1, 0)),
+    ((4, 0, 2), (0, 1, 1), (0, 1, 3)),
+    ((5, 0, 1), (5, 0, 3), (0, 1, 2)),
+    ((5, 0, 2), (1, 1, 0), (1, 1, 1), (1, 1, 3), (1, 1, 2)),
+)
+
+
 def plan_gather(agenda, net, layers, mats, count, load):
     far = net.ring.n // 2
 
-    def hop(j, h):
-        if h < far:
+    def hops(j, quarter):
+        for h in range(quarter * far // 4, (quarter + 1) * far // 4):
             net.arrived(j, h)
-        if h >= 1:
-            net.crossed(j, h - 1)
+        cross(j, quarter - 1)
+
+    def cross(j, quarter):
+        for h in range(max(quarter, 0) * far // 4, (quarter + 1) * far // 4):
+            net.crossed(j, h)
 
     def complete(j):
+        cross(j, 3)
         net.swapped(j)
         load(j).start()
 
-    agenda.add(0, net.own, 0)
-    agenda.add(0, net.own, 1)
-    for h in range(far + 1):
-        agenda.add(0, hop, 0, h)
-        if h == 0:
-            agenda.add(0, net.own, 3)
-        if h == 1:
-            agenda.add(0, net.own, 2)
-    agenda.add(0, complete, 0)
-    for h in range(far + 1):
-        for j in (1, 3, 2):
-            agenda.add(min(1 + h, count), hop, j, h)
-    for j in range(mats, layers * mats):
-        agenda.add(max(count - 2, 0), net.own, j)
-    for j in (1, 3, 2):
-        agenda.add(count, complete, j)
-    for k in range(1, layers):
-        start = (2 * k - 1) * count
-        for h in range(far + 1):
-            for j in range(k * mats, k * mats + mats):
-                agenda.add(start + 1 + min(h, count - 1), hop, j, h)
-        agenda.add(start + count, complete, k * mats)
-        for j in range(k * mats + 1, k * mats + mats):
-            agenda.add(start + count + 1, complete, j)
+    for k in range(layers):
+        for q, calls in enumerate((LATER if k else FIRST) + SECOND):
+            for what, ahead, m in calls:
+                if k + ahead < layers:
+                    j = (k + ahead) * mats + m
+                    when = 2 * count * k + q * count // 4
+                    if what == 0:
+                        agenda.add(when, net.own, j)
+                    elif what == 5:
+                        agenda.add(when, complete, j)
+                    else:
+                        agenda.add(when, hops, j, what - 1)
 
 
 def forward_kernel(n, n_seq, layers, rows, paired, *refs):

time: 349 us -> 328 us (0.940)
  Pallas kernels: 330 us -> 309 us
    pallas_call x1, Pallas kernels: 144 us -> 121 us  [run_forward(): pl.pallas_call(functools.partial(forward_kernel, n, n_seq, layers, rows,...]
where the time goes in v1:
time: 328 us; the launch traced here: 327 us
  Pallas kernels  309 us (94%)
  other arithmetic  10 us (3%)
  local copies, waits for them, and re-layouts  7.93 us (2%)
    pallas_call x1, Pallas kernels, run_forward(): pl.pallas_call(functools.partial(forward_kernel, n, n_seq, layers, rows,...  121 us
    pallas_call x1, Pallas kernels, grads_and_scatter(): pl.pallas_call(functools.partial(grads_kernel, n, plan), out_shape=[outs[...  117 us
    pallas_call x1, Pallas kernels, run_backward(): pl.pallas_call(functools.partial(backward_kernel, n_seq, layers, rows, ma...  70.6 us
    convert_element_type x4, other arithmetic, shards(): o.astype(F32)  6.89 us

profile of v1, /device:TPU:0, one launch (start us, length us, event | category | flops | bytes accessed | tf_op | source)
XLA Modules:
  0.0 327.2 jit_solution(16518258533403730306)
XLA Ops:
  0.6 1.2 broadcast_subtract_fusion.refs_0_
  1.9 0.8 fusion.4
  2.7 0.7 copy.17
  3.4 0.6 pad.4.refs_6_.refs_10_
  4.0 0.1 fusion
  4.2 0.7 stack.9.refs_7_.refs_11_
  4.8 120.9 %shard_map.152 = (bf16[768,1920]{1,0:T(8,128)(2,1)}, bf16[768,768]{1,0:T(8,128)(2,1)}, bf16[768,3072]{1,0:T(8,128)(2,1)}, bf16[1536,768]{1,0:T(8,128)(2,1)}, bf1...) custom-call(s32[2,6]{1,0:T(2,128)} %broadcast_subtract_fusion.refs_0, ...), custom_call_target="tpu_custom_call" | custom-call | tf_op jit(solution)/shard_map/pallas_call | solution.py:719
  125.8 70.6 %shard_map.153 = (bf16[2,1024,768]{2,1,0:T(8,128)(2,1)}, bf16[2,1024,3072]{2,1,0:T(8,128)(2,1)}, bf16[2,1024,768]{2,1,0:T(8,128)(2,1)}, bf16[2,1024,1920]{2,1,0:...) custom-call(s32[2,6]{1,0:T(2,128)} %broadcast_subtract_fusion.refs_0_, bf16[1024,768]{1,0:T(8,128)(2,1)} %bitcast.10, ...), custom_call_target="tpu_custom_call" | custom-call | tf_op jit(solution)/shard_map/pallas_call | solution.py:884
  196.4 1.0 bitcast_reduce_fusion
  197.4 0.6 reshape.42.refs_16_
  198.0 116.9 %shard_map.154 = (bf16[2,96,1920]{2,1,0:T(8,128)(2,1)}, bf16[2,96,768]{2,1,0:T(8,128)(2,1)}, bf16[2,96,3072]{2,1,0:T(8,128)(2,1)}, bf16[2,192,768]{2,1,0:T(8,128)(2,1)}, f32[8,768]{1,0:T(8,128)}) custom-call(bf16[2,1024,768]{2,1,0:T(8,128)(2,1)} %get-tuple-element.56.refs_0_.refs_7_, bf16[2,1024,768]{2,1,0:T(8,128)(2,1)} %get-tuple-element.57.refs_1_.refs_5_, ...), custom_call_target="tpu_custom_call" | custom-call | tf_op jit(solution)/shard_map/pallas_call | solution.py:1196
  315.0 0.0 copy-start.3
  315.0 0.0 copy-start.2
  315.0 0.9 reshape.43
  315.9 0.6 reshape_squeeze.3
  316.5 0.6 copy.19
  317.1 1.8 convert_element_type.15
  319.0 2.3 convert_element_type.14
  321.3 1.1 convert_element_type.17
  322.4 0.0 copy-done.2
  322.4 1.7 convert_element_type.16
  324.0 1.1 copy.22
  325.2 0.3 copy-done
  325.5 1.7 copy.23
  (6 shorter events, 0.1 us)
Async XLA Ops:
  315.0 6.3 %copy-start.3 = (bf16[2,192,768]{2,1,0:T(8,128)(2,1)S(1)}, bf16[2,192,768]{2,1,0:T(8,128)(2,1)}, u32[]{:S(2)}) copy-start(bf16[2,192,768]{2,1,0:T(8,128)(2,1)} %get-tuple-element.68) | copy-start | bytes 1769476
  315.0 7.4 %copy-start.2 = (bf16[2,96,3072]{2,1,0:T(8,128)(2,1)S(1)}, bf16[2,96,3072]{2,1,0:T(8,128)(2,1)}, u32[]{:S(2)}) copy-start(bf16[2,96,3072]{2,1,0:T(8,128)(2,1)} %get-tuple-element.67) | copy-start | bytes 3538948
  321.3 2.8 copy-start.1
  322.4 3.1 copy-start

commit v2 on v1

--- a/solution.py
+++ b/solution.py
@@ -1,4 +1,5 @@
 import functools
+import math
 
 import jax
 import jax.numpy as jnp
@@ -63,20 +64,20 @@
     return jnp.where(there == (here & 7) * (tokens // 8) + (here >> 3), 1.0, 0.0).astype(BF16)
 
 
-def reset_mask(rel_ref, row, first, tokens):
+def reset_mask(doc_ref, row, first, tokens):
     here = lax.broadcasted_iota(jnp.int32, (tokens, LANES), 0)
     pos = (here & 7) * (tokens // 8) + (here >> 3) + first
-    hit = pos == rel_ref[row, 0]
-    for k in range(1, rel_ref.shape[1]):
-        hit = hit | (pos == rel_ref[row, k])
+    hit = pos == doc_ref[row, 0]
+    for k in range(1, doc_ref.shape[1]):
+        hit = hit | (pos == doc_ref[row, k])
     return hit
 
 
-def retain(rel_ref, row, first, p_f, lower):
+def retain(doc_ref, row, first, p_f, lower):
     tokens, chan = p_f.shape
     forget = sigmoid(p_f)
     lam = lower + (1.0 - lower) * forget
-    keep = jnp.where(reset_mask(rel_ref, row, first, tokens), 0.0, 1.0)
+    keep = jnp.where(reset_mask(doc_ref, row, first, tokens), 0.0, 1.0)
     return lam * jnp.concatenate([keep] * (chan // LANES), axis=-1), forget, keep
 
 
@@ -93,7 +94,7 @@
     return pl.ds(pl.multiple_of(s * 8, 8), 8)
 
 
-def enter_tile(rel_ref, row, tile, x, w_ref, gain_ref, gate_ref, proj_ref, pg_ref, normed_ref, h_ref, cum_ref,
+def enter_tile(doc_ref, row, tile, start, x, w_ref, gain_ref, gate_ref, proj_ref, pg_ref, normed_ref, h_ref, cum_ref,
                ends_ref, tot_ref, src, lam_ref):
     tokens, width = x.shape
     chan = width // 2
@@ -106,7 +107,7 @@
     proj_ref[:, 2 * chan :] = p_f.astype(BF16)
     cos, sin, lower = gate_ref[0:1, :], gate_ref[1:2, :], gate_ref[2:3, :]
     seg_cos, seg_sin = gate_ref[3:4, :], gate_ref[4:5, :]
-    lam, _, _ = retain(rel_ref, row, tile * tokens, p_f, lower)
+    lam, _, _ = retain(doc_ref, row, start, p_f, lower)
     split_store(lam_ref, 0, lam)
     pg_ref[...] = dot(normed, w_ref[:, 3 * chan :]).astype(BF16)
     proj_ref[:, : 2 * chan] = p_c.astype(BF16)
@@ -221,7 +222,7 @@
     return mid + dot(hid_ref[...], wd_ref[...])
 
 
-def back_out_tile(rel_ref, row, tile, last, dx_ref, gu_ref, mid_ref, state_ref, pg_ref, pf_ref, wo_ref, wf_ref,
+def back_out_tile(doc_ref, row, tile, start, last, dx_ref, gu_ref, mid_ref, state_ref, pg_ref, pf_ref, wo_ref, wf_ref,
                   wd_ref, gain_ref, gate_ref, dz_ref, dgu_ref, dy_ref, dpg_ref, lam_ref, g_ref, cum_ref, ends_ref,
                   tot_ref, small_ref, grad):
     tokens, width = dx_ref.shape
@@ -269,7 +270,7 @@
     small_ref[8:16, :] += eight_sum(d_n * hat)
     d_hat = d_n * g1
     split_store(grad, 0, scale * (d_hat - hat * jnp.mean(d_hat * hat, axis=-1, keepdims=True)))
-    lam, _, _ = retain(rel_ref, row, tile * tokens, pf_ref[...].astype(F32), lower)
+    lam, _, _ = retain(doc_ref, row, start, pf_ref[...].astype(F32), lower)
     split_store(lam_ref, 0, lam)
     cos_l, sin_l = lanes(cos), lanes(sin)
 
@@ -313,7 +314,7 @@
     tot_ref[2:3, :] = c_l
 
 
-def back_in_tile(rel_ref, row, tile, last, dx_ref, x_ref, proj_ref, dpg_ref, lam_ref, starts_ref, state_ref, g_ref,
+def back_in_tile(doc_ref, row, tile, start, last, dx_ref, x_ref, proj_ref, dpg_ref, lam_ref, starts_ref, state_ref, g_ref,
                  cum_ref, ends_ref, carry_ref, w_ref, gain_ref, gate_ref, dproj_ref, small_ref, run):
     tokens, width = dx_ref.shape
     chan = width // 2
@@ -350,15 +351,15 @@
             after.append((w_r * cos_l[k] + w_i * sin_l[k], w_i * cos_l[k] - w_r * sin_l[k]))
         return tuple(after)
 
-    starts = (jnp.concatenate(l_r, axis=0), jnp.concatenate(l_i, axis=0))
-    lax.fori_loop(0, seg, step, tuple(zip(lanes(starts[0]), lanes(starts[1]))), unroll=8)
+    start_at = (jnp.concatenate(l_r, axis=0), jnp.concatenate(l_i, axis=0))
+    lax.fori_loop(0, seg, step, tuple(zip(lanes(start_at[0]), lanes(start_at[1]))), unroll=8)
     d_n = dot_t(dpg_ref[...], w_ref[:, 3 * chan :])
     g_r, g_i = wide(g_ref, 0, groups), wide(g_ref, groups, 2 * groups)
     prior = jnp.concatenate([starts_ref[...], state_ref[...].astype(F32)[: tokens - 8, :]], axis=0)
     q_r, q_i = prior[:, :chan], prior[:, chan:]
     p_r = proj_ref[:, :chan].astype(F32)
     p_i = proj_ref[:, chan : 2 * chan].astype(F32)
-    _, forget, keep = retain(rel_ref, row, tile * tokens, proj_ref[:, 2 * chan :].astype(F32), lower)
+    _, forget, keep = retain(doc_ref, row, start, proj_ref[:, 2 * chan :].astype(F32), lower)
     lam = wide(lam_ref, 0, groups)
     d_ar = g_r * q_r + g_i * q_i
     d_ai = g_i * q_r - g_r * q_i
@@ -391,21 +392,20 @@
 
 def combine(count, me, forward, buf, rot_ref, out_ref):
     cos, sin = rot_ref[0:1, :], rot_ref[1:2, :]
-    for r in range(buf.shape[1]):
-        c_r = jnp.zeros_like(cos)
-        c_i = jnp.zeros_like(cos)
-        for k in range(count - 1, 0, -1):
-            slot = k - 1 if forward else count - k - 1
-            valid = me >= k if forward else me + k < count
-            e_r, e_i, m = buf[slot, r, 0:1, :], buf[slot, r, 1:2, :], buf[slot, r, 2:3, :]
-            a_r = m * cos
-            a_i = m * sin if forward else -m * sin
-            n_r = a_r * c_r - a_i * c_i + e_r
-            n_i = a_r * c_i + a_i * c_r + e_i
-            keep = jnp.where(valid, 1.0, 0.0)
-            c_r, c_i = n_r * keep, n_i * keep
-        out_ref[r, 0:1, :] = c_r
-        out_ref[r, 1:2, :] = c_i
+    c_r = jnp.zeros_like(cos)
+    c_i = jnp.zeros_like(cos)
+    for k in range(count - 1, 0, -1):
+        slot = k - 1 if forward else count - k - 1
+        valid = me >= k if forward else me + k < count
+        e_r, e_i, m = buf[slot, 0:1, :], buf[slot, 1:2, :], buf[slot, 2:3, :]
+        a_r = m * cos
+        a_i = m * sin if forward else -m * sin
+        n_r = a_r * c_r - a_i * c_i + e_r
+        n_i = a_r * c_i + a_i * c_r + e_i
+        keep = jnp.where(valid, 1.0, 0.0)
+        c_r, c_i = n_r * keep, n_i * keep
+    out_ref[0:1, :] = c_r
+    out_ref[1:2, :] = c_i
 
 
 def carry_copies(count, me, tot_ref, buf, send_sem, recv_sem):
@@ -585,10 +585,9 @@
 
 
 def forward_kernel(n, n_seq, layers, rows, paired, *refs):
-    rel_ref, tok_ref = refs[:2]
+    doc_ref, tok_ref = refs[:2]
     mats = 4
-    given, (gain_ref, gate_ref) = refs[2 : 2 + mats], refs[2 + mats : 4 + mats]
-    refs = refs[4 + mats :]
+    given, table_ref, refs = refs[2 : 2 + mats], refs[2 + mats], refs[3 + mats :]
     if paired:
         gathered, refs = refs[: layers * mats], refs[layers * mats :]
     (xin_ref, proj_ref, pg_ref, normed_ref, starts_ref, state_ref, mixed_ref, mid_ref, normed2_ref, gu_ref, hid_ref,
@@ -596,7 +595,7 @@
     (xs, hs, cum, pg, ends, tot, src, lam, run, carry, buf, *rest) = refs[12:]
     weights, (load_sem, carry_send, carry_recv), sems = rest[:mats], rest[mats : mats + 3], rest[mats + 3 :]
     layer, step = pl.program_id(0), pl.program_id(1)
-    tokens = tok_ref.shape[0]
+    tokens, width = tok_ref.shape
     count = xs.shape[0]
     tiles = count // rows
     now = layer * (2 * count) + step
@@ -610,9 +609,6 @@
 
     def ready(j):
         load(j).wait()
-
-    def exchange():
-        return carry_copies(n_seq, me, tot, buf.at[layer], carry_send.at[layer], carry_recv.at[layer])
 
     if paired:
         ring = Ring(n)
@@ -637,7 +633,8 @@
 
     tile = lax.rem(step, count)
     row, at_row = tile // tiles, lax.rem(tile, tiles)
-    gains, gate = gain_ref.at[layer], gate_ref.at[layer]
+    start = (me * tiles + at_row) * tokens
+    gains, gate = table_ref.at[layer, 0:8], table_ref.at[layer, 8:16, 0 : width // 2]
 
     @pl.when((layer == 0) & (step < count))
     def _():
@@ -647,20 +644,23 @@
     def _():
         x = xs[tile]
         xin_ref[...] = x.astype(BF16)
-        enter_tile(rel_ref, row, at_row, x, weights[0], gains, gate, proj_ref, pg.at[tile], normed_ref, hs.at[tile],
+        enter_tile(doc_ref, row, at_row, start, x, weights[0], gains, gate, proj_ref, pg.at[tile], normed_ref, hs.at[tile],
                    cum.at[tile], ends.at[tile], tot.at[row], src, lam)
         pg_ref[...] = pg[tile]
 
-    @pl.when(step == count - 1)
+    def exchange():
+        return carry_copies(n_seq, me, tot.at[row], buf.at[layer, row], carry_send.at[layer, row], carry_recv.at[layer, row])
+
+    @pl.when((step < count) & (lax.rem(step, tiles) == tiles - 1))
     def _():
         for copy in exchange():
             copy.start()
 
-    @pl.when(step == count)
+    @pl.when((step >= count) & (lax.rem(step, tiles) == 0))
     def _():
         for copy in exchange():
             copy.wait()
-        combine(n_seq, me, True, buf.at[layer], gate.at[5:8], carry)
+        combine(n_seq, me, True, buf.at[layer, row], gate.at[5:8], carry.at[row])
 
     @pl.when(step >= count)
     def _():
@@ -691,7 +691,7 @@
     return flat, few
 
 
-def run_forward(n, n_seq, paired, rows, tokens, rel, x, sources, gain_rows, gate_rows):
+def run_forward(n, n_seq, paired, rows, tokens, docs, x, sources, table):
     layers = sources[0].shape[0]
     total, width = x.shape
     chan = width // 2
@@ -724,7 +724,7 @@
             pl.BlockSpec((tokens, width), lambda k, s: (jnp.where(k == 0, first(s), count - 1), 0)),
         ]
         + [any_] * mats
-        + [whole(layers, 8, width), whole(layers, 8, chan)],
+        + [whole(*table.shape)],
         out_specs=[any_] * jobs
         + [
             flat(width, first),
@@ -766,26 +766,26 @@
             pltpu.VMEM((chan // LANES, tokens, LANES), F32),
             pltpu.VMEM((8, chan), F32),
             pltpu.VMEM((rows, 8, chan), F32),
-            pltpu.VMEM((layers, n_seq - 1, rows, 8, chan), F32),
+            pltpu.VMEM((layers, rows, n_seq - 1, 8, chan), F32),
         ]
         + [pltpu.VMEM(f, BF16) for f in full]
-        + [dma((mats,)), dma((layers, n_seq - 1)), dma((layers, n_seq - 1))]
+        + [dma((mats,)), dma((layers, rows, n_seq - 1)), dma((layers, rows, n_seq - 1))]
         + [dma((s,)) if one else dma((s, n - 1)) for s in [max(jobs, 1)] for one in (1, 1, 0, 1, 0, 1, 1)],
         compiler_params=pltpu.CompilerParams(collective_id=3, has_side_effects=True, vmem_limit_bytes=LIMIT),
-    )(rel, x, *sources, gain_rows, gate_rows)
+    )(docs, x, *sources, table)
     return outs[:jobs], outs[jobs:]
 
 
 def backward_kernel(n_seq, layers, rows, mats, *refs):
-    rel_ref, cot_ref = refs[:2]
+    doc_ref, cot_ref = refs[:2]
     given, refs = refs[2 : 2 + layers * mats], refs[2 + layers * mats :]
-    (gain_ref, gate_ref, gu_ref, mid_ref, state_ref, pg_ref, pf_ref, x_ref, proj_ref, starts_ref, prior_ref, dz_ref,
-     dgu_ref, dy_ref, dproj_ref, dtok_ref, small_ref) = refs[:17]
-    (dxs, gs, cum, lam, dpg, ends, tot, grad, run, carry, buf, *rest) = refs[17:]
+    (table_ref, gu_ref, mid_ref, state_ref, pg_ref, pf_ref, x_ref, proj_ref, starts_ref, prior_ref, dz_ref,
+     dgu_ref, dy_ref, dproj_ref, dtok_ref, small_ref) = refs[:16]
+    (dxs, gs, cum, lam, dpg, ends, tot, grad, run, carry, buf, *rest) = refs[16:]
     weights, (load_sem, carry_send, carry_recv) = rest[:mats], rest[mats:]
     turn, step = pl.program_id(0), pl.program_id(1)
     layer = layers - 1 - turn
-    tokens = cot_ref.shape[0]
+    tokens, width = cot_ref.shape
     count = dxs.shape[0]
     tiles = count // rows
     now = turn * (2 * count) + step
@@ -795,32 +795,30 @@
     def load(t, m):
         return pltpu.make_async_copy(given[(layers - 1 - t) * mats + m], weights[m], load_sem.at[m])
 
-    def start(t, m):
+    def fetch(t, m):
         load(t, m).start()
 
     def ready(t, m):
         load(t, m).wait()
 
-    def exchange():
-        return carry_copies(n_seq, me, tot, buf.at[turn], carry_send.at[turn], carry_recv.at[turn])
-
     for m in (3, 2, 1):
-        agenda.add(0, start, 0, m)
+        agenda.add(0, fetch, 0, m)
     agenda.add(0, meet, [{"seq": lax.rem(me + k, n_seq)} for k in range(1, n_seq)])
     for t in range(layers):
         begin = 2 * count * t
-        agenda.add(begin, start, t, 0)
+        agenda.add(begin, fetch, t, 0)
         for m in (3, 2, 1):
             agenda.add(begin, ready, t, m)
         agenda.add(begin + count, ready, t, 0)
         if t + 1 < layers:
             for m in (3, 2, 1):
-                agenda.add(begin + count, start, t + 1, m)
+                agenda.add(begin + count, fetch, t + 1, m)
     agenda.run(now)
 
     tile = count - 1 - lax.rem(step, count)
     row, at_row = tile // tiles, lax.rem(tile, tiles)
-    gains, gate = gain_ref.at[layer], gate_ref.at[layer]
+    start = (me * tiles + at_row) * tokens
+    gains, gate = table_ref.at[layer, 0:8], table_ref.at[layer, 8:16, 0 : width // 2]
 
     @pl.when(step == 0)
     def _():
@@ -832,24 +830,27 @@
 
     @pl.when(step < count)
     def _():
-        back_out_tile(rel_ref, row, at_row, tiles - 1, dxs.at[tile], gu_ref, mid_ref, state_ref, pg_ref, pf_ref,
+        back_out_tile(doc_ref, row, at_row, start, tiles - 1, dxs.at[tile], gu_ref, mid_ref, state_ref, pg_ref, pf_ref,
                       weights[1], weights[2], weights[3], gains, gate, dz_ref, dgu_ref, dy_ref, dpg.at[tile],
                       lam.at[tile], gs.at[tile], cum.at[tile], ends.at[tile], tot.at[row], small_ref, grad)
 
-    @pl.when(step == count - 1)
+    def exchange():
+        return carry_copies(n_seq, me, tot.at[row], buf.at[turn, row], carry_send.at[turn, row], carry_recv.at[turn, row])
+
+    @pl.when((step < count) & (lax.rem(step, tiles) == tiles - 1))
     def _():
         for copy in exchange():
             copy.start()
 
-    @pl.when(step == count)
+    @pl.when((step >= count) & (lax.rem(step, tiles) == 0))
     def _():
         for copy in exchange():
             copy.wait()
-        combine(n_seq, me, False, buf.at[turn], gate.at[5:8], carry)
+        combine(n_seq, me, False, buf.at[turn, row], gate.at[5:8], carry.at[row])
 
     @pl.when(step >= count)
     def _():
-        back_in_tile(rel_ref, row, at_row, tiles - 1, dxs.at[tile], x_ref, proj_ref, dpg.at[tile], lam.at[tile],
+        back_in_tile(doc_ref, row, at_row, start, tiles - 1, dxs.at[tile], x_ref, proj_ref, dpg.at[tile], lam.at[tile],
                      starts_ref, prior_ref, gs.at[tile], cum.at[tile], ends.at[tile], carry.at[row], weights[0],
                      gains, gate, dproj_ref, small_ref, run)
 
@@ -862,7 +863,7 @@
             dtok_ref[...] = dot(order, high) + dot(order, low)
 
 
-def run_backward(n_seq, rows, tokens, rel, cotangent, weights, gain_rows, gate_rows, kept):
+def run_backward(n_seq, rows, tokens, docs, cotangent, weights, table, kept):
     x, proj, p_g, starts, state, mid, gu = kept
     layers, total, width = x.shape
     chan = width // 2
@@ -890,8 +891,7 @@
         ]
         + [any_] * len(weights)
         + [
-            whole(layers, 8, width),
-            whole(layers, 8, chan),
+            whole(*table.shape),
             flat(2 * hidden, first),
             flat(width, first),
             flat(width, first),
@@ -929,12 +929,12 @@
             pltpu.VMEM((width // LANES, tokens, LANES), F32),
             pltpu.VMEM((8, chan), F32),
             pltpu.VMEM((rows, 8, chan), F32),
-            pltpu.VMEM((layers, n_seq - 1, rows, 8, chan), F32),
+            pltpu.VMEM((layers, rows, n_seq - 1, 8, chan), F32),
         ]
         + [pltpu.VMEM(w.shape, BF16) for w in weights[:mats]]
-        + [dma((mats,)), dma((layers, n_seq - 1)), dma((layers, n_seq - 1))],
+        + [dma((mats,)), dma((layers, rows, n_seq - 1)), dma((layers, rows, n_seq - 1))],
         compiler_params=pltpu.CompilerParams(collective_id=2, has_side_effects=True, vmem_limit_bytes=LIMIT),
-    )(rel, cotangent, *weights, gain_rows, gate_rows, gu, mid, state, p_g, proj, x, proj, starts, state)
+    )(docs, cotangent, *weights, table, gu, mid, state, p_g, proj, x, proj, starts, state)
 
 
 def add_rows(dst, dst_row, parts, rows):
@@ -954,8 +954,8 @@
     jobs = len(plan)
     lefts, rights, small = refs[:jobs], refs[jobs : 2 * jobs], refs[2 * jobs]
     outs_count = 1 + max(p[0] for p in plan)
-    outs, small_out = refs[2 * jobs + 1 : 2 * jobs + 1 + outs_count], refs[2 * jobs + 1 + outs_count]
-    rest = refs[2 * jobs + 2 + outs_count :]
+    outs, rest = refs[2 * jobs + 1 : 2 * jobs + 1 + outs_count], refs[2 * jobs + 1 + outs_count :]
+    gains_out, gate_out, rest = rest[0], rest[1], rest[2:]
     grads, core_buf, y_buf, ring_buf, fin_buf = (rest[i * jobs : (i + 1) * jobs] for i in range(5))
     (left_big, left_small, right_buf, small_buf, left_sem, right_sem, core_send, core_recv, y_send, y_recv,
      ring_send, ring_recv, end_send, end_recv, small_send, small_recv) = rest[5 * jobs :]
@@ -1028,7 +1028,10 @@
     def small_round(r):
         return remote(small_buf.at[2 * r], small_buf.at[2 * r + 1], small_send.at[r], small_recv.at[r], rounds[r])
 
-    small_buf[0] = small[...]
+    layers = small.shape[0]
+    for k in range(layers):
+        for i in range(4):
+            small_buf[0, 4 * k + i : 4 * k + i + 1, :] = jnp.sum(small[k, 8 * i : 8 * i + 8, :], axis=0, keepdims=True)
     small_round(0).start()
 
     def small_step(r):
@@ -1038,7 +1041,11 @@
             small_buf[2 * r + 2] = total
             small_round(r + 1).start()
         else:
-            small_out[...] = total
+            chan = gate_out.shape[2]
+            for k in range(layers):
+                gains_out[k] = total[4 * k : 4 * k + 3, :]
+                gate_out[k, 0:1, :] = total[4 * k + 3 : 4 * k + 4, :chan]
+                gate_out[k, 1:2, :] = total[4 * k + 3 : 4 * k + 4, chan:]
 
     def begin(j):
         for slot, (way, h, dist) in enumerate(order):
@@ -1182,7 +1189,7 @@
     jobs = len(plan)
     plan = [p + (a.shape[2], b.shape[2]) for p, a, b in zip(plan, lefts, rights)]
     tokens = lefts[0].shape[1]
-    layers = 1 + max(p[1] for p in plan)
+    layers, _, width = small.shape
     dma = pltpu.SemaphoreType.DMA
     rounds = 2 + (n - 1).bit_length()
     sizes = [(p[3] // n // 6, p[4], p[2]) for p in plan]
@@ -1195,9 +1202,10 @@
 
     return pl.pallas_call(
         functools.partial(grads_kernel, n, plan),
-        out_shape=[outs[m] for m in sorted(outs)] + [jax.ShapeDtypeStruct(small.shape, F32)],
+        out_shape=[outs[m] for m in sorted(outs)]
+        + [jax.ShapeDtypeStruct((layers, 3, width), F32), jax.ShapeDtypeStruct((layers, 2, width // 2), F32)],
         in_specs=[any_] * (2 * jobs) + [vm],
-        out_specs=[vm] * (len(outs) + 1),
+        out_specs=[vm] * (len(outs) + 2),
         scratch_shapes=bufs(lambda u, w, s: (6 * u * n, w))
         + bufs(lambda u, w, s: (n, 3 * u, w))
         + bufs(lambda u, w, s: (n if s else 1, u, w))
@@ -1207,7 +1215,7 @@
             pltpu.VMEM((tokens, max(p[3] for p in plan[0::2])), BF16),
             pltpu.VMEM((tokens, max(p[3] for p in plan[1::2])), BF16),
             pltpu.VMEM((2, tokens, CHUNK), BF16),
-            pltpu.VMEM((2 * rounds,) + small.shape, F32),
+            pltpu.VMEM((2 * rounds, 4 * layers, width), F32),
             dma((2,)), dma((2,)), dma((jobs,)), dma((jobs, n)), dma((jobs,)), dma((jobs, n)), dma((jobs,)),
             dma((jobs, n)), dma((jobs, 2)), dma((jobs, 2)), dma((rounds,)), dma((rounds,)),
         ],
@@ -1235,33 +1243,32 @@
     n, n_seq = lax.axis_size("batch"), lax.axis_size("seq")
     sources = (mixer_in, mixer_out, ffn_in, ffn_out)
     paired = n_seq == 4 and n % 4 == 0 and all(w.shape[1] % 96 == 0 for w in sources)
-    rel = doc_starts - lax.axis_index("seq") * length
-    gain_rows = jnp.pad(gains, ((0, 0), (0, 5), (0, 0)))
-    theta, lower = gate_params[:, 0], gate_params[:, 1]
-    turns = jnp.stack([theta, theta * seg, theta * length], axis=1)
-    cos, sin = jnp.cos(turns), jnp.sin(turns)
-    gate_rows = jnp.stack(
-        [cos[:, 0], sin[:, 0], lower, cos[:, 1], sin[:, 1], cos[:, 2], sin[:, 2], lower], axis=1
+    theta, lower = gate_params[:, 0:1], gate_params[:, 1:2]
+    at = lax.broadcasted_iota(jnp.int32, (layers, 8, chan), 1)
+    times = jnp.where(at < 3, 1, jnp.where(at < 5, seg, length)).astype(F32)
+    quarter = jnp.where((at == 1) | (at == 4) | (at == 6), math.pi / 2, 0.0)
+    gate_rows = jnp.where(at == 2, lower, jnp.cos(theta * times - quarter))
+    table = jnp.concatenate(
+        [jnp.pad(gains, ((0, 0), (0, 5), (0, 0))), jnp.pad(gate_rows, ((0, 0), (0, 0), (0, width - chan)))], axis=1
     )
     x = tokens_in.reshape(total, width)
     if paired:
-        weights, kept = run_forward(n, n_seq, True, rows, tokens, rel, x, sources, gain_rows, gate_rows)
+        weights, kept = run_forward(n, n_seq, True, rows, tokens, doc_starts, x, sources, table)
     else:
         stacked = [lax.all_gather(w, "batch", axis=1, tiled=True) for w in sources]
         weights = [w[k] for k in range(layers) for w in stacked]
-        _, kept = run_forward(n, n_seq, False, rows, tokens, rel, x, stacked, gain_rows, gate_rows)
+        _, kept = run_forward(n, n_seq, False, rows, tokens, doc_starts, x, stacked, table)
     x_in, proj, p_g, normed, starts, state, mixed, mid, normed2, gu, hid, block_out = kept
     dz, d_gu, dy, d_proj, d_tokens, small = run_backward(
-        n_seq, rows, tokens, rel, cotangent.reshape(total, width), weights, gain_rows, gate_rows,
+        n_seq, rows, tokens, doc_starts, cotangent.reshape(total, width), weights, table,
         (x_in, proj, p_g, starts, state, mid, gu),
     )
-    small = jnp.sum(small.reshape(layers, 4, 8, width), axis=2).reshape(layers * 4, width)
     pairs = ((normed, d_proj), (mixed, dy), (normed2, d_gu), (hid, dz))
     if paired:
         plan = []
         for k in reversed(range(layers)):
             plan += [(m, k, m != 0) for m in ((1, 2, 3, 0) if k == layers - 1 else (3, 2, 0, 1))]
-        *outs, totals = grads_and_scatter(
+        *outs, d_gains, d_gate = grads_and_scatter(
             n, plan, [pairs[m][0] for m, _, _ in plan], [pairs[m][1] for m, _, _ in plan], small
         )
     else:
@@ -1270,14 +1277,14 @@
             whole_grads = jnp.stack([contract_rows(left[k], right[k]) for k in range(layers)])
             part = lax.psum_scatter(whole_grads, "batch", scatter_dimension=1, tiled=True)
             outs.append(lax.psum(part, "seq"))
-        totals = lax.psum(small, ("batch", "seq"))
-    totals = totals.reshape(layers, 4, width)
+        totals = lax.psum(jnp.sum(small.reshape(layers, 4, 8, width), axis=2), ("batch", "seq"))
+        d_gains, d_gate = totals[:, :3], totals[:, 3].reshape(layers, 2, chan)
     return (
         block_out.reshape(rows, length, width),
         d_tokens.reshape(rows, length, width),
         *[o.astype(F32) for o in outs],
-        totals[:, :3],
-        totals[:, 3].reshape(layers, 2, chan),
+        d_gains,
+        d_gate,
     )
 
 

time: 328 us -> 318 us (0.970)
  Pallas kernels: 309 us -> 302 us
    pallas_call x1, Pallas kernels: 70.6 us -> 65.6 us  [run_backward(): pl.pallas_call(functools.partial(backward_kernel, n_seq, layers, rows, ma...]
where the time goes in v2:
time: 318 us
  Pallas kernels  302 us (95%)
  other arithmetic  7.72 us (2%)
  local copies, waits for them, and re-layouts  6.74 us (2%)
    pallas_call x1, Pallas kernels, run_forward(): pl.pallas_call(functools.partial(forward_kernel, n, n_seq, layers, rows,...  119 us
    pallas_call x1, Pallas kernels, grads_and_scatter(): pl.pallas_call(functools.partial(grads_kernel, n, plan), out_shape=[outs[...  117 us
    pallas_call x1, Pallas kernels, run_backward(): pl.pallas_call(functools.partial(backward_kernel, n_seq, layers, rows, ma...  65.6 us
    convert_element_type x4, other arithmetic, shards(): o.astype(F32)  6.89 us

profile of v2, /device:TPU:0, one launch (start us, length us, event | category | flops | bytes accessed | tf_op | source)
XLA Modules:
  0.0 317.6 jit_solution(15575129364127865000)
XLA Ops:
  0.7 0.8 fusion
  1.5 0.2 cosine_select_fusion
  1.6 0.7 copy.19
  2.4 0.6 select_maximum_fusion.refs_6_.refs_10_
  3.0 119.5 %shard_map.152 = (bf16[768,1920]{1,0:T(8,128)(2,1)}, bf16[768,768]{1,0:T(8,128)(2,1)}, bf16[768,3072]{1,0:T(8,128)(2,1)}, bf16[1536,768]{1,0:T(8,128)(2,1)}, bf1...) custom-call(s32[2,6]{1,0:T(2,128)} %refs_0_.3, ...), custom_call_target="tpu_custom_call" | custom-call | tf_op jit(solution)/shard_map/pallas_call | solution.py:719
  122.5 65.6 %shard_map.153 = (bf16[2,1024,768]{2,1,0:T(8,128)(2,1)}, bf16[2,1024,3072]{2,1,0:T(8,128)(2,1)}, bf16[2,1024,768]{2,1,0:T(8,128)(2,1)}, bf16[2,1024,1920]{2,1,0:...) custom-call(s32[2,6]{1,0:T(2,128)} %refs_0_.3, bf16[1024,768]{1,0:T(8,128)(2,1)} %bitcast.11, ...), custom_call_target="tpu_custom_call" | custom-call | tf_op jit(solution)/shard_map/pallas_call | solution.py:885
  188.1 117.4 %shard_map.154 = (bf16[2,96,1920]{2,1,0:T(8,128)(2,1)}, bf16[2,96,768]{2,1,0:T(8,128)(2,1)}, bf16[2,96,3072]{2,1,0:T(8,128)(2,1)}, bf16[2,192,768]{2,1,0:T(8,128...) custom-call(bf16[2,1024,768]{2,1,0:T(8,128)(2,1)} %get-tuple-element.57.refs_0_.refs_7_, ...), custom_call_target="tpu_custom_call" | custom-call | tf_op jit(solution)/shard_map/pallas_call | solution.py:1203
  305.5 0.0 copy-start.3
  305.5 0.0 copy-start.2
  305.5 1.5 copy.20
  307.0 1.8 convert_element_type.21
  308.8 2.3 convert_element_type.20
  311.1 0.0 copy-done.3
  311.1 0.0 copy-start.1
  311.1 1.1 convert_element_type.23
  312.2 0.0 copy-done.2
  312.2 0.0 copy-start
  312.2 1.7 convert_element_type.22
  313.9 0.0 copy-done.1
  313.9 1.1 copy.28
  315.0 0.3 copy-done
  315.4 1.7 copy.29
  317.1 0.0 copy-done.4
  317.1 0.6 copy.30
  (5 shorter events, 0.0 us)
Async XLA Ops:
  305.5 5.6 %copy-start.3 = (bf16[2,192,768]{2,1,0:T(8,128)(2,1)S(1)}, bf16[2,192,768]{2,1,0:T(8,128)(2,1)}, u32[]{:S(2)}) copy-start(bf16[2,192,768]{2,1,0:T(8,128)(2,1)} %get-tuple-element.69) | copy-start | bytes 1769476
  305.5 6.7 %copy-start.2 = (bf16[2,96,3072]{2,1,0:T(8,128)(2,1)S(1)}, bf16[2,96,3072]{2,1,0:T(8,128)(2,1)}, u32[]{:S(2)}) copy-start(bf16[2,96,3072]{2,1,0:T(8,128)(2,1)} %get-tuple-element.68) | copy-start | bytes 3538948
  311.1 2.8 copy-start.1
  312.2 3.1 copy-start
  315.4 1.7 copy-start.4

commit v3 on v2

--- a/solution.py
+++ b/solution.py
@@ -13,6 +13,7 @@
 BF16 = jnp.bfloat16
 LANES = 128
 CHUNK = 768
+ORDERS = (((1, 0, 1), (2, 0, 2), (3, 0, 1), (2, 1, 2), (0, 0, 1)), ((2, 0, 2), (3, 0, 1), (2, 1, 2), (0, 0, 1), (1, 0, 1)))
 MESH = pl.DeviceIdType.MESH
 
 
@@ -671,7 +672,7 @@
 
         @pl.when(layer == layers - 1)
         def _():
-            out_ref[...] = dot(order_matrix(tokens, True), out.astype(BF16)).astype(BF16)
+            out_ref[...] = out.astype(BF16)
 
     if paired:
 
@@ -856,11 +857,7 @@
 
         @pl.when(turn == layers - 1)
         def _():
-            dx = dxs[tile]
-            high = dx.astype(BF16)
-            low = (dx - high.astype(F32)).astype(BF16)
-            order = order_matrix(tokens, True)
-            dtok_ref[...] = dot(order, high) + dot(order, low)
+            dtok_ref[...] = dxs[tile]
 
 
 def run_backward(n_seq, rows, tokens, docs, cotangent, weights, table, kept):
@@ -977,7 +974,7 @@
         return pltpu.make_async_copy(lefts[j].at[plan[j][1]], buf.at[:, 0 : plan[j][3]], left_sem.at[j % 2])
 
     chunks = []
-    for j, (_, _, _, rows, cols) in enumerate(plan):
+    for j, (_, _, _, rows, cols, _, _) in enumerate(plan):
         first = 0
         while first < cols:
             size = min(CHUNK, cols - first)
@@ -987,7 +984,7 @@
     def right_copy(i):
         j, first, size, _ = chunks[i]
         return pltpu.make_async_copy(
-            rights[j].at[plan[j][1], :, first : first + size], right_buf.at[i % 2, :, 0:size], right_sem.at[i % 2]
+            rights[j].at[plan[j][1], :, plan[j][5] + first : plan[j][5] + first + size], right_buf.at[i % 2, :, 0:size], right_sem.at[i % 2]
         )
 
     left_copy(0).start()
@@ -1092,14 +1089,17 @@
         return remote(rows_at(grads[j], mine(j, ring.batch), own_rows[j]), fin_buf[j], end_send.at[j, 0],
                       end_recv.at[j, 0], y_dev)
 
+    def out_of(j):
+        return outs[plan[j][0]].at[plan[j][1], :, plan[j][5] : plan[j][5] + plan[j][4]]
+
     def half_copy(j):
-        half = outs[plan[j][0]].at[plan[j][1], pl.ds(pl.multiple_of(core * (3 * us[j]), 16), 3 * us[j])]
+        half = out_of(j).at[pl.ds(pl.multiple_of(core * (3 * us[j]), 16), 3 * us[j])]
         return remote(half, half, end_send.at[j, 1], end_recv.at[j, 1], core_dev)
 
     def finish(j):
         u = us[j]
         fin_copy(j).wait_recv()
-        out = outs[plan[j][0]].at[plan[j][1]]
+        out = out_of(j)
         at, to = mine(j, ring.batch), core * (3 * u)
         if split[j]:
             add_rows(out, to + 2 * y * u, [(grads[j], at + y * u)], u)
@@ -1187,13 +1187,17 @@
 
 def grads_and_scatter(n, plan, lefts, rights, small):
     jobs = len(plan)
-    plan = [p + (a.shape[2], b.shape[2]) for p, a, b in zip(plan, lefts, rights)]
+    full = []
+    for (m, k, crosses, part, of), a, b in zip(plan, lefts, rights):
+        cols = b.shape[2] // of
+        full.append((m, k, crosses, a.shape[2], cols, part * cols, b.shape[2]))
+    plan = full
     tokens = lefts[0].shape[1]
     layers, _, width = small.shape
     dma = pltpu.SemaphoreType.DMA
     rounds = 2 + (n - 1).bit_length()
     sizes = [(p[3] // n // 6, p[4], p[2]) for p in plan]
-    outs = {p[0]: jax.ShapeDtypeStruct((layers, p[3] // n, p[4]), BF16) for p in plan}
+    outs = {p[0]: jax.ShapeDtypeStruct((layers, p[3] // n, p[6]), BF16) for p in plan}
     vm = pl.BlockSpec(memory_space=pltpu.VMEM)
     any_ = pl.BlockSpec(memory_space=pl.ANY)
 
@@ -1223,6 +1227,42 @@
             collective_id=4, has_side_effects=True, vmem_limit_bytes=63 * 1024 * 1024
         ),
     )(*lefts, *rights, small)
+
+
+def finish_kernel(mats, *refs):
+    grads, (out_ref, dtok_ref) = refs[:mats], refs[mats : mats + 2]
+    wide_refs, (out_to, dtok_to) = refs[mats + 2 : 2 * mats + 2], refs[2 * mats + 2 :]
+    for grad, to in zip(grads, wide_refs):
+        to[...] = grad[...].astype(F32)
+    order = order_matrix(out_ref.shape[0], True)
+    out_to[...] = dot(order, out_ref[...]).astype(BF16)
+    dx = dtok_ref[...]
+    high = dx.astype(BF16)
+    dtok_to[...] = dot(order, high) + dot(order, (dx - high.astype(F32)).astype(BF16))
+
+
+def finish(tokens, grads, block_out, d_tokens):
+    total, width = block_out.shape
+    count = total // tokens
+    if grads[0].shape[0] * 2 != count:
+        def ordered(values):
+            return values.reshape(count, tokens // 8, 8, width).swapaxes(1, 2).reshape(total, width)
+
+        return [g.astype(F32) for g in grads], ordered(block_out), ordered(d_tokens)
+    halves = [
+        pl.BlockSpec((1, g.shape[1] // 2, g.shape[2]), lambda i: (i // 2, i % 2, 0)) for g in grads
+    ]
+    tile = pl.BlockSpec((tokens, width), lambda i: (i, 0))
+    outs = pl.pallas_call(
+        functools.partial(finish_kernel, len(grads)),
+        grid=(count,),
+        in_specs=halves + [tile, tile],
+        out_specs=halves + [tile, tile],
+        out_shape=[jax.ShapeDtypeStruct(g.shape, F32) for g in grads]
+        + [jax.ShapeDtypeStruct(v.shape, v.dtype) for v in (block_out, d_tokens)],
+        compiler_params=pltpu.CompilerParams(vmem_limit_bytes=LIMIT),
+    )(*grads, block_out, d_tokens)
+    return outs[:-2], outs[-2], outs[-1]
 
 
 def contract_rows(left, right):
@@ -1267,9 +1307,10 @@
     if paired:
         plan = []
         for k in reversed(range(layers)):
-            plan += [(m, k, m != 0) for m in ((1, 2, 3, 0) if k == layers - 1 else (3, 2, 0, 1))]
+            jobs = ORDERS[0] if k == layers - 1 else ORDERS[1]
+            plan += [(m, k, m != 0, part, of) for m, part, of in jobs]
         *outs, d_gains, d_gate = grads_and_scatter(
-            n, plan, [pairs[m][0] for m, _, _ in plan], [pairs[m][1] for m, _, _ in plan], small
+            n, plan, [pairs[p[0]][0] for p in plan], [pairs[p[0]][1] for p in plan], small
         )
     else:
         outs = []
@@ -1279,10 +1320,11 @@
             outs.append(lax.psum(part, "seq"))
         totals = lax.psum(jnp.sum(small.reshape(layers, 4, 8, width), axis=2), ("batch", "seq"))
         d_gains, d_gate = totals[:, :3], totals[:, 3].reshape(layers, 2, chan)
+    outs, block_out, d_tokens = finish(tokens, outs, block_out, d_tokens)
     return (
         block_out.reshape(rows, length, width),
         d_tokens.reshape(rows, length, width),
-        *[o.astype(F32) for o in outs],
+        *outs,
         d_gains,
         d_gate,
     )

time: 318 us -> 312 us (0.981)
  other arithmetic: 7.72 us -> 0.83 us
  Pallas kernels: 302 us -> 307 us
  local copies, waits for them, and re-layouts: 6.74 us -> 3.46 us
    pallas_call x0 -> x1, Pallas kernels: none -> 7.82 us  [finish(): pl.pallas_call(functools.partial(finish_kernel, len(grads)), grid=(count,...]
    convert_element_type x4 -> x0, other arithmetic: 6.89 us -> none  [shards(): o.astype(F32)]
    unnamed x16 -> x6, local copies, waits for them, and re-layouts: 5.97 us -> 2.69 us
where the time goes in v3:
time: 312 us
  Pallas kernels  307 us (98%)
  local copies, waits for them, and re-layouts  3.46 us (1%)
    pallas_call x1, Pallas kernels, run_forward(): pl.pallas_call(functools.partial(forward_kernel, n, n_seq, layers, rows,...  119 us
    pallas_call x1, Pallas kernels, grads_and_scatter(): pl.pallas_call(functools.partial(grads_kernel, n, plan), out_shape=[outs[...  116 us
    pallas_call x1, Pallas kernels, run_backward(): pl.pallas_call(functools.partial(backward_kernel, n_seq, layers, rows, ma...  64.2 us
    pallas_call x1, Pallas kernels, finish(): pl.pallas_call(functools.partial(finish_kernel, len(grads)), grid=(count,...  7.82 us

profile of v3, /device:TPU:0, one launch (start us, length us, event | category | flops | bytes accessed | tf_op | source)
XLA Modules:
  0.0 311.7 jit_solution(5541936673328255631)
XLA Ops:
  0.7 0.8 fusion
  1.5 0.2 cosine_select_fusion
  1.6 0.7 copy.19
  2.4 0.6 select_maximum_fusion.refs_6_.refs_10_
  3.0 118.6 %shard_map.152 = (bf16[768,1920]{1,0:T(8,128)(2,1)}, bf16[768,768]{1,0:T(8,128)(2,1)}, bf16[768,3072]{1,0:T(8,128)(2,1)}, bf16[1536,768]{1,0:T(8,128)(2,1)}, bf1...) custom-call(s32[2,6]{1,0:T(2,128)} %refs_0_.3, ...), custom_call_target="tpu_custom_call" | custom-call | tf_op jit(solution)/shard_map/pallas_call | solution.py:720
  121.7 64.2 %shard_map.153 = (bf16[2,1024,768]{2,1,0:T(8,128)(2,1)}, bf16[2,1024,3072]{2,1,0:T(8,128)(2,1)}, bf16[2,1024,768]{2,1,0:T(8,128)(2,1)}, bf16[2,1024,1920]{2,1,0:...) custom-call(s32[2,6]{1,0:T(2,128)} %refs_0_.3, bf16[1024,768]{1,0:T(8,128)(2,1)} %bitcast.9, ...), custom_call_target="tpu_custom_call" | custom-call | tf_op jit(solution)/shard_map/pallas_call | solution.py:882
  185.8 116.0 %shard_map.154 = (bf16[2,96,1920]{2,1,0:T(8,128)(2,1)}, bf16[2,96,768]{2,1,0:T(8,128)(2,1)}, bf16[2,96,3072]{2,1,0:T(8,128)(2,1)}, bf16[2,192,768]{2,1,0:T(8,128...) custom-call(bf16[2,1024,768]{2,1,0:T(8,128)(2,1)} %get-tuple-element.46.refs_0_.refs_9_, ...), custom_call_target="tpu_custom_call" | custom-call | tf_op jit(solution)/shard_map/pallas_call | solution.py:1207
  301.9 1.4 copy.20
  303.2 0.0 copy-start
  303.2 7.8 %shard_map.155 = (f32[2,96,1920]{2,1,0:T(8,128)}, f32[2,96,768]{2,1,0:T(8,128)}, f32[2,96,3072]{2,1,0:T(8,128)}, f32[2,192,768]{2,1,0:T(8,128)}, bf16[1024,768]{1,0:T(8,128)(2,1)}, /*index=5*/f32[1024,768]{1,0:T(8,128)}) custom-call(bf16[2,96,1920]{2,1,0:T(8,128)(2,1)} %get-tuple-element.70.refs_0_, bf16[2,96,768]{2,1,0:T(8,128)(2,1)} %get-tuple-element.71.refs_1_, ...), custom_call_target="tpu_custom_call" | custom-call | tf_op jit(solution)/shard_map/pallas_call | solution.py:1256
  311.1 0.0 copy-done
  311.1 0.6 copy.26
  (4 shorter events, 0.0 us)
Async XLA Ops:
  303.2 7.8 %copy-start = (f32[2,2,384]{2,1,0:T(2,128)S(1)}, f32[2,2,384]{2,1,0:T(2,128)}, u32[]{:S(2)}) copy-start(f32[2,2,384]{2,1,0:T(2,128)} %get-tuple-element.121) | copy-start | bytes 18436

commit v4 on v3

--- a/solution.py
+++ b/solution.py
@@ -549,12 +549,12 @@
     ((5, 0, 0), (3, 0, 2)),
     ((4, 0, 1), (4, 0, 3), (0, 1, 0)),
     ((4, 0, 2), (0, 1, 1), (0, 1, 3)),
-    ((5, 0, 1), (5, 0, 3), (0, 1, 2)),
-    ((5, 0, 2), (1, 1, 0), (1, 1, 1), (1, 1, 3), (1, 1, 2)),
+    ((5, 0, 1), (5, 0, 3), (5, 0, 2), (0, 1, 2)),
+    ((1, 1, 0), (1, 1, 1), (1, 1, 3), (1, 1, 2)),
 )
 
 
-def plan_gather(agenda, net, layers, mats, count, load):
+def plan_gather(agenda, net, layers, mats, count, load, save):
     far = net.ring.n // 2
 
     def hops(j, quarter):
@@ -569,7 +569,13 @@
     def complete(j):
         cross(j, 3)
         net.swapped(j)
-        load(j).start()
+        if j < mats:
+            save(j).start()
+        else:
+            if j < 2 * mats:
+                save(j - mats).wait()
+                net.sent(j - mats)
+            load(j).start()
 
     for k in range(layers):
         for q, calls in enumerate((LATER if k else FIRST) + SECOND):
@@ -594,7 +600,7 @@
     (xin_ref, proj_ref, pg_ref, normed_ref, starts_ref, state_ref, mixed_ref, mid_ref, normed2_ref, gu_ref, hid_ref,
      out_ref) = refs[:12]
     (xs, hs, cum, pg, ends, tot, src, lam, run, carry, buf, *rest) = refs[12:]
-    weights, (load_sem, carry_send, carry_recv), sems = rest[:mats], rest[mats : mats + 3], rest[mats + 3 :]
+    weights, (load_sem, save_sem, carry_send, carry_recv), sems = rest[:mats], rest[mats : mats + 4], rest[mats + 4 :]
     layer, step = pl.program_id(0), pl.program_id(1)
     tokens, width = tok_ref.shape
     count = xs.shape[0]
@@ -614,19 +620,23 @@
     if paired:
         ring = Ring(n)
         jobs = [
-            (given[m].at[k], gathered[k * mats + m], given[m].shape[1] // 6)
+            (given[m].at[k], gathered[k * mats + m] if k else weights[m], given[m].shape[1] // 6)
             for k in range(layers) for m in range(mats)
         ]
         net = Gather(ring, jobs, sems)
+
+        def save(j):
+            return pltpu.make_async_copy(weights[j], gathered[j], save_sem.at[j])
+
         agenda.add(0, meet, [{"batch": ring.ahead(1)}, {"batch": ring.ahead(-1)}] + peers)
-        plan_gather(agenda, net, layers, mats, count, load)
+        plan_gather(agenda, net, layers, mats, count, load, save)
     else:
         agenda.add(0, meet, peers)
         for k in range(layers):
             agenda.add(2 * count * k, lambda k=k: load(k * mats).start())
             for m in range(1, mats):
                 agenda.add(2 * count * k + count - 1, lambda j=k * mats + m: load(j).start())
-    for k in range(layers):
+    for k in range(1 if paired else 0, layers):
         agenda.add(2 * count * k, ready, k * mats)
         for m in range(1, mats):
             agenda.add(2 * count * k + count, ready, k * mats + m)
@@ -679,7 +689,10 @@
         @pl.when(now == layers * 2 * count - 1)
         def _():
             for j in range(layers * mats):
-                net.sent(j)
+                if j < mats and layers == 1:
+                    save(j).wait()
+                if j >= mats or layers == 1:
+                    net.sent(j)
 
 
 def tile_specs(tokens, layer):
@@ -770,7 +783,7 @@
             pltpu.VMEM((layers, rows, n_seq - 1, 8, chan), F32),
         ]
         + [pltpu.VMEM(f, BF16) for f in full]
-        + [dma((mats,)), dma((layers, rows, n_seq - 1)), dma((layers, rows, n_seq - 1))]
+        + [dma((mats,)), dma((mats,)), dma((layers, rows, n_seq - 1)), dma((layers, rows, n_seq - 1))]
         + [dma((s,)) if one else dma((s, n - 1)) for s in [max(jobs, 1)] for one in (1, 1, 0, 1, 0, 1, 1)],
         compiler_params=pltpu.CompilerParams(collective_id=3, has_side_effects=True, vmem_limit_bytes=LIMIT),
     )(docs, x, *sources, table)

time: 312 us -> 305 us (0.978)
  Pallas kernels: 307 us -> 300 us
    pallas_call x1, Pallas kernels: 119 us -> 113 us  [run_forward(): pl.pallas_call(functools.partial(forward_kernel, n, n_seq, layers, rows,...]
where the time goes in v4:
time: 305 us
  Pallas kernels  300 us (98%)
  local copies, waits for them, and re-layouts  3.46 us (1%)
    pallas_call x1, Pallas kernels, grads_and_scatter(): pl.pallas_call(functools.partial(grads_kernel, n, plan), out_shape=[outs[...  115 us
    pallas_call x1, Pallas kernels, run_forward(): pl.pallas_call(functools.partial(forward_kernel, n, n_seq, layers, rows,...  113 us
    pallas_call x1, Pallas kernels, run_backward(): pl.pallas_call(functools.partial(backward_kernel, n_seq, layers, rows, ma...  64.2 us
    pallas_call x1, Pallas kernels, finish(): pl.pallas_call(functools.partial(finish_kernel, len(grads)), grid=(count,...  7.81 us

profile of v4, /device:TPU:0, one launch (start us, length us, event | category | flops | bytes accessed | tf_op | source)
XLA Modules:
  0.0 304.6 jit_solution(15686310673567506150)
XLA Ops:
  0.7 0.8 fusion
  1.5 0.2 cosine_select_fusion
  1.6 0.7 copy.19
  2.4 0.6 select_maximum_fusion.refs_6_.refs_10_
  3.0 112.9 %shard_map.152 = (bf16[768,1920]{1,0:T(8,128)(2,1)}, bf16[768,768]{1,0:T(8,128)(2,1)}, bf16[768,3072]{1,0:T(8,128)(2,1)}, bf16[1536,768]{1,0:T(8,128)(2,1)}, bf1...) custom-call(s32[2,6]{1,0:T(2,128)} %refs_0_.3, ...), custom_call_target="tpu_custom_call" | custom-call | tf_op jit(solution)/shard_map/pallas_call | solution.py:733
  115.9 64.2 %shard_map.153 = (bf16[2,1024,768]{2,1,0:T(8,128)(2,1)}, bf16[2,1024,3072]{2,1,0:T(8,128)(2,1)}, bf16[2,1024,768]{2,1,0:T(8,128)(2,1)}, bf16[2,1024,1920]{2,1,0:...) custom-call(s32[2,6]{1,0:T(2,128)} %refs_0_.3, bf16[1024,768]{1,0:T(8,128)(2,1)} %bitcast.9, ...), custom_call_target="tpu_custom_call" | custom-call | tf_op jit(solution)/shard_map/pallas_call | solution.py:895
  180.1 114.8 %shard_map.154 = (bf16[2,96,1920]{2,1,0:T(8,128)(2,1)}, bf16[2,96,768]{2,1,0:T(8,128)(2,1)}, bf16[2,96,3072]{2,1,0:T(8,128)(2,1)}, bf16[2,192,768]{2,1,0:T(8,128...) custom-call(bf16[2,1024,768]{2,1,0:T(8,128)(2,1)} %get-tuple-element.46.refs_0_.refs_9_, ...), custom_call_target="tpu_custom_call" | custom-call | tf_op jit(solution)/shard_map/pallas_call | solution.py:1220
  294.8 1.4 copy.20
  296.2 0.0 copy-start
  296.2 7.8 %shard_map.155 = (f32[2,96,1920]{2,1,0:T(8,128)}, f32[2,96,768]{2,1,0:T(8,128)}, f32[2,96,3072]{2,1,0:T(8,128)}, f32[2,192,768]{2,1,0:T(8,128)}, bf16[1024,768]{1,0:T(8,128)(2,1)}, /*index=5*/f32[1024,768]{1,0:T(8,128)}) custom-call(bf16[2,96,1920]{2,1,0:T(8,128)(2,1)} %get-tuple-element.70.refs_0_, bf16[2,96,768]{2,1,0:T(8,128)(2,1)} %get-tuple-element.71.refs_1_, ...), custom_call_target="tpu_custom_call" | custom-call | tf_op jit(solution)/shard_map/pallas_call | solution.py:1269
  304.0 0.0 copy-done
  304.0 0.6 copy.26
  (4 shorter events, 0.0 us)
Async XLA Ops:
  296.2 7.8 %copy-start = (f32[2,2,384]{2,1,0:T(2,128)S(1)}, f32[2,2,384]{2,1,0:T(2,128)}, u32[]{:S(2)}) copy-start(f32[2,2,384]{2,1,0:T(2,128)} %get-tuple-element.121) | copy-start | bytes 18436

commit v5 on v4

--- a/solution.py
+++ b/solution.py
@@ -12,7 +12,7 @@
 F32 = jnp.float32
 BF16 = jnp.bfloat16
 LANES = 128
-CHUNK = 768
+CHUNK = 1024
 ORDERS = (((1, 0, 1), (2, 0, 2), (3, 0, 1), (2, 1, 2), (0, 0, 1)), ((2, 0, 2), (3, 0, 1), (2, 1, 2), (0, 0, 1), (1, 0, 1)))
 MESH = pl.DeviceIdType.MESH
 

time: 305 us -> 304 us (level)
  no operation moved by 1% of the time
where the time goes in v5:
time: 304 us; the launch traced here: 303 us
  Pallas kernels  298 us (98%)
  local copies, waits for them, and re-layouts  3.46 us (1%)
    pallas_call x1, Pallas kernels, grads_and_scatter(): pl.pallas_call(functools.partial(grads_kernel, n, plan), out_shape=[outs[...  114 us
    pallas_call x1, Pallas kernels, run_forward(): pl.pallas_call(functools.partial(forward_kernel, n, n_seq, layers, rows,...  113 us
    pallas_call x1, Pallas kernels, run_backward(): pl.pallas_call(functools.partial(backward_kernel, n_seq, layers, rows, ma...  64.2 us
    pallas_call x1, Pallas kernels, finish(): pl.pallas_call(functools.partial(finish_kernel, len(grads)), grid=(count,...  7.81 us

profile of v5, /device:TPU:0, one launch (start us, length us, event | category | flops | bytes accessed | tf_op | source)
XLA Modules:
  0.0 303.4 jit_solution(3204312926265427155)
XLA Ops:
  0.7 0.8 fusion
  1.5 0.2 cosine_select_fusion
  1.6 0.7 copy.19
  2.4 0.6 select_maximum_fusion.refs_6_.refs_10_
  3.0 112.9 %shard_map.152 = (bf16[768,1920]{1,0:T(8,128)(2,1)}, bf16[768,768]{1,0:T(8,128)(2,1)}, bf16[768,3072]{1,0:T(8,128)(2,1)}, bf16[1536,768]{1,0:T(8,128)(2,1)}, bf1...) custom-call(s32[2,6]{1,0:T(2,128)} %refs_0_.3, ...), custom_call_target="tpu_custom_call" | custom-call | tf_op jit(solution)/shard_map/pallas_call | solution.py:733
  115.9 64.2 %shard_map.153 = (bf16[2,1024,768]{2,1,0:T(8,128)(2,1)}, bf16[2,1024,3072]{2,1,0:T(8,128)(2,1)}, bf16[2,1024,768]{2,1,0:T(8,128)(2,1)}, bf16[2,1024,1920]{2,1,0:...) custom-call(s32[2,6]{1,0:T(2,128)} %refs_0_.3, bf16[1024,768]{1,0:T(8,128)(2,1)} %bitcast.9, ...), custom_call_target="tpu_custom_call" | custom-call | tf_op jit(solution)/shard_map/pallas_call | solution.py:895
  180.1 113.5 %shard_map.154 = (bf16[2,96,1920]{2,1,0:T(8,128)(2,1)}, bf16[2,96,768]{2,1,0:T(8,128)(2,1)}, bf16[2,96,3072]{2,1,0:T(8,128)(2,1)}, bf16[2,192,768]{2,1,0:T(8,128...) custom-call(bf16[2,1024,768]{2,1,0:T(8,128)(2,1)} %get-tuple-element.46.refs_0_.refs_9_, ...), custom_call_target="tpu_custom_call" | custom-call | tf_op jit(solution)/shard_map/pallas_call | solution.py:1220
  293.6 1.4 copy.20
  295.0 0.0 copy-start
  295.0 7.8 %shard_map.155 = (f32[2,96,1920]{2,1,0:T(8,128)}, f32[2,96,768]{2,1,0:T(8,128)}, f32[2,96,3072]{2,1,0:T(8,128)}, f32[2,192,768]{2,1,0:T(8,128)}, bf16[1024,768]{1,0:T(8,128)(2,1)}, /*index=5*/f32[1024,768]{1,0:T(8,128)}) custom-call(bf16[2,96,1920]{2,1,0:T(8,128)(2,1)} %get-tuple-element.70.refs_0_, bf16[2,96,768]{2,1,0:T(8,128)(2,1)} %get-tuple-element.71.refs_1_, ...), custom_call_target="tpu_custom_call" | custom-call | tf_op jit(solution)/shard_map/pallas_call | solution.py:1269
  302.8 0.0 copy-done
  302.8 0.6 copy.26
  (4 shorter events, 0.0 us)
Async XLA Ops:
  295.0 7.8 %copy-start = (f32[2,2,384]{2,1,0:T(2,128)S(1)}, f32[2,2,384]{2,1,0:T(2,128)}, u32[]{:S(2)}) copy-start(f32[2,2,384]{2,1,0:T(2,128)} %get-tuple-element.121) | copy-start | bytes 18436
